TPU v7x, 32 devices: a whole 2x2x4 slice. The times are simulated.
32 devices in a mesh: ctx: 16 (over z, x, core), tp: 2 (over y).
Axes of the slice: x: 2, y: 2, z: 4, core: 2. Of those that a mesh axis runs over, the one named last changes fastest.
Arguments:
- queries: bfloat16 [4096, 8192], P('ctx', 'tp'), may hold values from -8 to 8
- key_rows: bfloat16 [4096, 1024], P('ctx', 'tp'), may hold values from -8 to 8
- value_head_rows: bfloat16 [4096, 1024], P('ctx', 'tp'), may hold values from -6 to 6
- ssm_input: bfloat16 [4096, 8192], P('ctx', 'tp'), may hold values from -6 to 6
- gate_input: bfloat16 [4096, 8192], P('ctx', 'tp'), may hold values from -6 to 6
- b_matrix: bfloat16 [4096, 1024], P('ctx', 'tp'), may hold values from -6 to 6
- c_matrix: bfloat16 [4096, 1024], P('ctx', 'tp'), may hold values from -0.5 to 0.5
- step_size: float32 [128, 4096], P('tp', 'ctx'), may hold values from 0.02 to 0.2
- log_decay: float32 [128, 4096], P('tp', 'ctx'), may hold values from -1.5 to 0
- skip_gain: float32 [128], P('tp'), may hold values from 0.5 to 1.5
- norm_gain: bfloat16 [8192], P('tp'), may hold values from 0.099609375 to 1.8984375
Outputs:
- attention_out: bfloat16 [4096, 8192], P('ctx', 'tp')
- mixer_out: bfloat16 [4096, 8192], P('ctx', 'tp')
All inputs are finite; a program needn't handle non-finite values.
Results may differ from a plain program's by a relative error of at most 0.022.
Values may be sent and summed in bfloat16 or wider, within the bound.
A program may use at most 128 MiB of HBM per device.

v0:
```python
import math

import jax
import jax.numpy as jnp
from jax import lax
from jax.sharding import PartitionSpec as P

HEAD_WIDTH = 128
STATE_HEADS = 128
P_SIZE = 64
N = 128


causal_score = -1e30


def passed_along(block, axis, distance):
    devices = range(lax.axis_size(axis))
    route = [(i - distance, i) for i in devices if i - distance in devices]
    return lax.ppermute(block, axis, route)


def attend_rows(running_in, key_block, value_block, key_start, query_head_rows, query_pos):
    row_count = key_block.shape[0]
    sub_width = math.gcd(row_count, 512)
    kv_heads = query_head_rows.shape[1]
    score_factor = query_head_rows.shape[3] ** (-0.5)

    def sub_step(sub_id, running):
        run_max, run_sum, summed_so_far = running
        offset = sub_id * sub_width
        key_portion = key_block.reshape(sub_width, kv_heads, -1)
        value_portion = value_block.reshape(sub_width, kv_heads, -1)
        key_pos = key_start + offset + jnp.arange(sub_width, dtype=jnp.int32)
        is_valid = key_pos[None, :] <= query_pos[:, None]
        score_matrix = (
            jnp.einsum(
                "faqo,bao->aqfb", query_head_rows, key_portion, preferred_element_type=jnp.float32
            )
            * score_factor
        )
        score_matrix = jnp.where(is_valid, score_matrix, causal_score)
        new_max = jnp.maximum(run_max, jnp.max(score_matrix, axis=-1))
        weights = jnp.where(is_valid, jnp.exp(score_matrix - new_max[..., None]), 0.0)
        correction_factor = jnp.exp(run_max - new_max)
        run_sum = run_sum * correction_factor + jnp.sum(weights, axis=-1)
        summed_so_far = summed_so_far * correction_factor[..., None] + jnp.einsum(
            "wlhc,cwm->wlhm",
            weights.astype(jnp.bfloat16),
            value_portion,
            preferred_element_type=jnp.float32,
        )
        return (new_max, run_sum, summed_so_far)

    return lax.fori_loop(0, row_count // sub_width, sub_step, running_in)


def local(
    queries,
    key_rows,
    value_head_rows,
    ssm_input,
    gate_input,
    b_matrix,
    c_matrix,
    step_size,
    log_decay,
    skip_gain,
    norm_gain,
):
    tok_rows = queries.shape[0]
    kv_heads = key_rows.shape[1] // HEAD_WIDTH
    query_per_key_heads = queries.shape[1] // HEAD_WIDTH // kv_heads
    query_head_rows = queries.reshape(tok_rows, kv_heads, query_per_key_heads, HEAD_WIDTH)
    ctx_count = lax.axis_size("ctx")
    position = lax.axis_index("ctx")
    query_pos = position * tok_rows + jnp.arange(tok_rows, dtype=jnp.int32)
    starting_state = (
        jnp.full((kv_heads, query_per_key_heads, tok_rows), causal_score, jnp.float32),
        jnp.zeros((kv_heads, query_per_key_heads, tok_rows), jnp.float32),
        jnp.zeros((kv_heads, query_per_key_heads, tok_rows, HEAD_WIDTH), jnp.float32),
    )
    first_pass = attend_rows(
        starting_state, key_rows, value_head_rows, position * tok_rows, query_head_rows, query_pos
    )

    def cycle_step(step_id, state):
        stacked, running = state
        stacked = passed_along(stacked, "ctx", 1)
        sender_index = position - step_id
        key_start = jnp.where(sender_index >= 0, sender_index * tok_rows, ctx_count * tok_rows)
        return (
            stacked,
            attend_rows(running, stacked[0], stacked[1], key_start, query_head_rows, query_pos),
        )

    _, (run_max, run_sum, summed_so_far) = lax.fori_loop(
        1, ctx_count, cycle_step, (jnp.stack((key_rows, value_head_rows)), first_pass)
    )
    attention_out = (
        (summed_so_far / run_sum[..., None])
        .transpose(2, 0, 1, 3)
        .reshape(tok_rows, -1)
        .astype(jnp.bfloat16)
    )
    heads_local = step_size.shape[0]
    groups_local = b_matrix.shape[1] // N
    heads_group = heads_local // groups_local
    mixer_in = ssm_input.reshape(tok_rows, groups_local, heads_group, P_SIZE)
    in_maps = b_matrix.reshape(tok_rows, groups_local, N)
    out_maps = c_matrix.reshape(tok_rows, groups_local, N)
    steps_here = step_size.reshape(groups_local, heads_group, tok_rows)
    cumul = jnp.cumsum(log_decay.reshape(groups_local, heads_group, tok_rows), axis=-1)
    causal = jnp.tril(jnp.ones((tok_rows, tok_rows), dtype=bool))
    gram = jnp.einsum("tgn,sgn->gts", out_maps, in_maps, preferred_element_type=jnp.float32)
    spread = jnp.where(causal, cumul[..., :, None] - cumul[..., None, :], 0.0)
    mixing = jnp.where(
        causal, gram[:, None] * jnp.exp(spread) * steps_here[..., None, :], 0.0
    ).astype(jnp.bfloat16)
    inner = jnp.einsum("ghts,sghp->tghp", mixing, mixer_in, preferred_element_type=jnp.float32)
    weight_end = jnp.exp(cumul[..., -1:] - cumul) * steps_here
    weighted = (mixer_in * weight_end.transpose(2, 0, 1)[..., None]).astype(jnp.bfloat16)
    local_state = jnp.einsum(
        "sghp,sgn->ghpn", weighted, in_maps, preferred_element_type=jnp.float32
    )
    block_decay = jnp.exp(cumul[..., -1])

    def relay_step(step_id, pair):
        received, outgoing = pair
        received = passed_along(outgoing.astype(jnp.bfloat16), "ctx", 1).astype(outgoing.dtype)
        return (received, block_decay[..., None, None] * received + local_state)

    incoming, _ = lax.fori_loop(
        1, ctx_count, relay_step, (jnp.zeros_like(local_state), local_state)
    )
    carried_out = jnp.einsum(
        "ghpn,tgn->tghp", incoming, out_maps.astype(jnp.float32), precision=lax.Precision.HIGHEST
    )
    carried_out = carried_out * jnp.exp(cumul).transpose(2, 0, 1)[..., None]
    direct = skip_gain.reshape(groups_local, heads_group)[None, :, :, None] * mixer_in.astype(
        jnp.float32
    )
    outputs = (inner + carried_out + direct).reshape(tok_rows, -1)
    gated = outputs * jax.nn.silu(gate_input.astype(jnp.float32))
    square_total = lax.psum(jnp.sum(gated * gated, axis=-1), "tp")
    scaling = lax.rsqrt(square_total / (STATE_HEADS * P_SIZE) + 1e-05)
    mixer_out = (gated * scaling[:, None] * norm_gain.astype(jnp.float32)).astype(jnp.bfloat16)
    return (attention_out, mixer_out)


def solution(mesh):
    placed = (
        P("ctx", "tp"),
        P("ctx", "tp"),
        P("ctx", "tp"),
        P("ctx", "tp"),
        P("ctx", "tp"),
        P("ctx", "tp"),
        P("ctx", "tp"),
        P("tp", "ctx"),
        P("tp", "ctx"),
        P("tp"),
        P("tp"),
    )
    return jax.shard_map(
        local,
        mesh=mesh,
        in_specs=placed,
        out_specs=(P("ctx", "tp"), P("ctx", "tp")),
        check_vma=False,
    )
```

profile of v0, /device:TPU:24, one launch (start us, length us, event | category | flops | bytes accessed | tf_op | source)
XLA Modules:
  0.0 674.8 jit_solution(3861514806404055636)
XLA Ops:
  11.2 6.9 %broadcast_add_fusion = f32[4,8,256,128]{3,2,1,0:T(8,128)} fusion(f32[4,8,256]{2,1,0:T(8,128)S(1)} %get-tuple-element.324, f32[4,256,256,8]{2,1,3,0:T(8,128)} %copy-done, f32[4,8,256]{2,1,0:T(8,128)S(1)} %broadcast_maximum_fusion, pred[256,256]{0,1:T(8,128)(4,1)S(1)} %broadcast_compare_fusion.1, bf16[256,4,128,1]{2,1,0,3:T(4,128)(2,1)S(1)} %bitcast.128), kind=kOutput, calls=%fused_computation.59 | convolution fusion | flops 548405248 | bytes 12976128 | tf_op jit(solution)/shard_map/while/body/eval_jaxpr/wlhc,cwm->wlhm/dot_general | solution.py:47
  21.2 312.9 %while.55 = (s32[]{:T(128)}, bf16[2,256,512]{1,2,0:T(8,128)(2,1)S(1)}, f32[4,8,256]{2,1,0:T(8,128)S(1)}, f32[4,8,256]{2,1,0:T(8,128)S(1)}, f32[4,8,256,128]{3,2,...) while((s32[]{:T(128)}, ...), condition=%wide.region_5.6_spmd.clone, body=%wide.region_2.5_spmd.clone.sunk | while | flops 1103184384 | bytes 74715408 | solution.py:97
  23.3 9.3 %collective-permute-done.1 = bf16[2,256,512]{1,2,0:T(8,128)(2,1)S(1)} collective-permute-done((bf16[2,256,512]{1,2,0:T(8,128)(2,1)S(1)}, bf16[2,256,512]{1,2,0:T(8,128)(2,1)S(1)}, u32[]{:S(2)}, u32[]{:S(2)}) %collective-permute-start.1) | collective-permute-done | bytes 524320 | tf_op jit(solution)/shard_map/while/body/eval_jaxpr/ppermute | solution.py:20
  36.4 3.7 multiply_add_fusion.8
  44.1 9.3 %collective-permute-done.1 = bf16[2,256,512]{1,2,0:T(8,128)(2,1)S(1)} collective-permute-done((bf16[2,256,512]{1,2,0:T(8,128)(2,1)S(1)}, bf16[2,256,512]{1,2,0:T(8,128)(2,1)S(1)}, u32[]{:S(2)}, u32[]{:S(2)}) %collective-permute-start.1) | collective-permute-done | bytes 524320 | tf_op jit(solution)/shard_map/while/body/eval_jaxpr/ppermute | solution.py:20
  57.2 3.7 multiply_add_fusion.8
  65.0 9.3 %collective-permute-done.1 = bf16[2,256,512]{1,2,0:T(8,128)(2,1)S(1)} collective-permute-done((bf16[2,256,512]{1,2,0:T(8,128)(2,1)S(1)}, bf16[2,256,512]{1,2,0:T(8,128)(2,1)S(1)}, u32[]{:S(2)}, u32[]{:S(2)}) %collective-permute-start.1) | collective-permute-done | bytes 524320 | tf_op jit(solution)/shard_map/while/body/eval_jaxpr/ppermute | solution.py:20
  78.1 3.7 multiply_add_fusion.8
  85.9 9.3 %collective-permute-done.1 = bf16[2,256,512]{1,2,0:T(8,128)(2,1)S(1)} collective-permute-done((bf16[2,256,512]{1,2,0:T(8,128)(2,1)S(1)}, bf16[2,256,512]{1,2,0:T(8,128)(2,1)S(1)}, u32[]{:S(2)}, u32[]{:S(2)}) %collective-permute-start.1) | collective-permute-done | bytes 524320 | tf_op jit(solution)/shard_map/while/body/eval_jaxpr/ppermute | solution.py:20
  99.0 3.7 multiply_add_fusion.8
  106.7 9.3 %collective-permute-done.1 = bf16[2,256,512]{1,2,0:T(8,128)(2,1)S(1)} collective-permute-done((bf16[2,256,512]{1,2,0:T(8,128)(2,1)S(1)}, bf16[2,256,512]{1,2,0:T(8,128)(2,1)S(1)}, u32[]{:S(2)}, u32[]{:S(2)}) %collective-permute-start.1) | collective-permute-done | bytes 524320 | tf_op jit(solution)/shard_map/while/body/eval_jaxpr/ppermute | solution.py:20
  127.6 9.3 %collective-permute-done.1 = bf16[2,256,512]{1,2,0:T(8,128)(2,1)S(1)} collective-permute-done((bf16[2,256,512]{1,2,0:T(8,128)(2,1)S(1)}, bf16[2,256,512]{1,2,0:T(8,128)(2,1)S(1)}, u32[]{:S(2)}, u32[]{:S(2)}) %collective-permute-start.1) | collective-permute-done | bytes 524320 | tf_op jit(solution)/shard_map/while/body/eval_jaxpr/ppermute | solution.py:20
  148.4 9.3 %collective-permute-done.1 = bf16[2,256,512]{1,2,0:T(8,128)(2,1)S(1)} collective-permute-done((bf16[2,256,512]{1,2,0:T(8,128)(2,1)S(1)}, bf16[2,256,512]{1,2,0:T(8,128)(2,1)S(1)}, u32[]{:S(2)}, u32[]{:S(2)}) %collective-permute-start.1) | collective-permute-done | bytes 524320 | tf_op jit(solution)/shard_map/while/body/eval_jaxpr/ppermute | solution.py:20
  161.5 3.7 multiply_add_fusion.8
  169.3 9.3 %collective-permute-done.1 = bf16[2,256,512]{1,2,0:T(8,128)(2,1)S(1)} collective-permute-done((bf16[2,256,512]{1,2,0:T(8,128)(2,1)S(1)}, bf16[2,256,512]{1,2,0:T(8,128)(2,1)S(1)}, u32[]{:S(2)}, u32[]{:S(2)}) %collective-permute-start.1) | collective-permute-done | bytes 524320 | tf_op jit(solution)/shard_map/while/body/eval_jaxpr/ppermute | solution.py:20
  182.4 3.7 multiply_add_fusion.8
  190.1 9.3 %collective-permute-done.1 = bf16[2,256,512]{1,2,0:T(8,128)(2,1)S(1)} collective-permute-done((bf16[2,256,512]{1,2,0:T(8,128)(2,1)S(1)}, bf16[2,256,512]{1,2,0:T(8,128)(2,1)S(1)}, u32[]{:S(2)}, u32[]{:S(2)}) %collective-permute-start.1) | collective-permute-done | bytes 524320 | tf_op jit(solution)/shard_map/while/body/eval_jaxpr/ppermute | solution.py:20
  211.0 9.3 %collective-permute-done.1 = bf16[2,256,512]{1,2,0:T(8,128)(2,1)S(1)} collective-permute-done((bf16[2,256,512]{1,2,0:T(8,128)(2,1)S(1)}, bf16[2,256,512]{1,2,0:T(8,128)(2,1)S(1)}, u32[]{:S(2)}, u32[]{:S(2)}) %collective-permute-start.1) | collective-permute-done | bytes 524320 | tf_op jit(solution)/shard_map/while/body/eval_jaxpr/ppermute | solution.py:20
  224.1 3.7 multiply_add_fusion.8
  231.8 9.3 %collective-permute-done.1 = bf16[2,256,512]{1,2,0:T(8,128)(2,1)S(1)} collective-permute-done((bf16[2,256,512]{1,2,0:T(8,128)(2,1)S(1)}, bf16[2,256,512]{1,2,0:T(8,128)(2,1)S(1)}, u32[]{:S(2)}, u32[]{:S(2)}) %collective-permute-start.1) | collective-permute-done | bytes 524320 | tf_op jit(solution)/shard_map/while/body/eval_jaxpr/ppermute | solution.py:20
  245.0 3.7 multiply_add_fusion.8
  252.7 9.3 %collective-permute-done.1 = bf16[2,256,512]{1,2,0:T(8,128)(2,1)S(1)} collective-permute-done((bf16[2,256,512]{1,2,0:T(8,128)(2,1)S(1)}, bf16[2,256,512]{1,2,0:T(8,128)(2,1)S(1)}, u32[]{:S(2)}, u32[]{:S(2)}) %collective-permute-start.1) | collective-permute-done | bytes 524320 | tf_op jit(solution)/shard_map/while/body/eval_jaxpr/ppermute | solution.py:20
  273.6 9.3 %collective-permute-done.1 = bf16[2,256,512]{1,2,0:T(8,128)(2,1)S(1)} collective-permute-done((bf16[2,256,512]{1,2,0:T(8,128)(2,1)S(1)}, bf16[2,256,512]{1,2,0:T(8,128)(2,1)S(1)}, u32[]{:S(2)}, u32[]{:S(2)}) %collective-permute-start.1) | collective-permute-done | bytes 524320 | tf_op jit(solution)/shard_map/while/body/eval_jaxpr/ppermute | solution.py:20
  286.7 3.7 multiply_add_fusion.8
  294.4 9.3 %collective-permute-done.1 = bf16[2,256,512]{1,2,0:T(8,128)(2,1)S(1)} collective-permute-done((bf16[2,256,512]{1,2,0:T(8,128)(2,1)S(1)}, bf16[2,256,512]{1,2,0:T(8,128)(2,1)S(1)}, u32[]{:S(2)}, u32[]{:S(2)}) %collective-permute-start.1) | collective-permute-done | bytes 524320 | tf_op jit(solution)/shard_map/while/body/eval_jaxpr/ppermute | solution.py:20
  307.5 3.7 multiply_add_fusion.8
  315.3 9.3 %collective-permute-done.1 = bf16[2,256,512]{1,2,0:T(8,128)(2,1)S(1)} collective-permute-done((bf16[2,256,512]{1,2,0:T(8,128)(2,1)S(1)}, bf16[2,256,512]{1,2,0:T(8,128)(2,1)S(1)}, u32[]{:S(2)}, u32[]{:S(2)}) %collective-permute-start.1) | collective-permute-done | bytes 524320 | tf_op jit(solution)/shard_map/while/body/eval_jaxpr/ppermute | solution.py:20
  350.2 288.4 %while.54 = (s32[]{:T(128)}, f32[4,16,64,128]{3,2,1,0:T(8,128)}, bf16[4,16,64,128]{3,2,1,0:T(8,128)(2,1)}, f32[4,16]{1,0:T(4,128)S(1)}, f32[4,16,64,128]{3,2,1,0:T(8,128)S(1)}, /*index=5*/s32[]{:T(128)}) while((s32[]{:T(128)}, f32[4,16,64,128]{3,2,1,0:T(8,128)}, bf16[4,16,64,128]{3,2,1,0:T(8,128)(2,1)}, f32[4,16]{1,0:T(4,128)S(1)}, ...), condition=%wide.region_9.10_spmd, body=%wide.region_8.9_spmd.sunk | while | flops 2097154 | bytes 10486125 | solution.py:133
  352.2 15.3 %collective-permute-done = bf16[4,16,64,128]{3,2,1,0:T(8,128)(2,1)S(1)} collective-permute-done((bf16[4,16,64,128]{3,2,1,0:T(8,128)(2,1)}, bf16[4,16,64,128]{3,2,1,0:T(8,128)(2,1)S(1)}, u32[]{:S(2)}, u32[]{:S(2)}) %collective-permute-start) | collective-permute-done | bytes 1048608 | tf_op jit(solution)/shard_map/while/body/eval_jaxpr/ppermute | solution.py:20
  371.4 15.3 %collective-permute-done = bf16[4,16,64,128]{3,2,1,0:T(8,128)(2,1)S(1)} collective-permute-done((bf16[4,16,64,128]{3,2,1,0:T(8,128)(2,1)}, bf16[4,16,64,128]{3,2,1,0:T(8,128)(2,1)S(1)}, u32[]{:S(2)}, u32[]{:S(2)}) %collective-permute-start) | collective-permute-done | bytes 1048608 | tf_op jit(solution)/shard_map/while/body/eval_jaxpr/ppermute | solution.py:20
  390.6 15.3 %collective-permute-done = bf16[4,16,64,128]{3,2,1,0:T(8,128)(2,1)S(1)} collective-permute-done((bf16[4,16,64,128]{3,2,1,0:T(8,128)(2,1)}, bf16[4,16,64,128]{3,2,1,0:T(8,128)(2,1)S(1)}, u32[]{:S(2)}, u32[]{:S(2)}) %collective-permute-start) | collective-permute-done | bytes 1048608 | tf_op jit(solution)/shard_map/while/body/eval_jaxpr/ppermute | solution.py:20
  409.8 15.3 %collective-permute-done = bf16[4,16,64,128]{3,2,1,0:T(8,128)(2,1)S(1)} collective-permute-done((bf16[4,16,64,128]{3,2,1,0:T(8,128)(2,1)}, bf16[4,16,64,128]{3,2,1,0:T(8,128)(2,1)S(1)}, u32[]{:S(2)}, u32[]{:S(2)}) %collective-permute-start) | collective-permute-done | bytes 1048608 | tf_op jit(solution)/shard_map/while/body/eval_jaxpr/ppermute | solution.py:20
  429.1 15.3 %collective-permute-done = bf16[4,16,64,128]{3,2,1,0:T(8,128)(2,1)S(1)} collective-permute-done((bf16[4,16,64,128]{3,2,1,0:T(8,128)(2,1)}, bf16[4,16,64,128]{3,2,1,0:T(8,128)(2,1)S(1)}, u32[]{:S(2)}, u32[]{:S(2)}) %collective-permute-start) | collective-permute-done | bytes 1048608 | tf_op jit(solution)/shard_map/while/body/eval_jaxpr/ppermute | solution.py:20
  448.3 15.3 %collective-permute-done = bf16[4,16,64,128]{3,2,1,0:T(8,128)(2,1)S(1)} collective-permute-done((bf16[4,16,64,128]{3,2,1,0:T(8,128)(2,1)}, bf16[4,16,64,128]{3,2,1,0:T(8,128)(2,1)S(1)}, u32[]{:S(2)}, u32[]{:S(2)}) %collective-permute-start) | collective-permute-done | bytes 1048608 | tf_op jit(solution)/shard_map/while/body/eval_jaxpr/ppermute | solution.py:20
  467.5 15.3 %collective-permute-done = bf16[4,16,64,128]{3,2,1,0:T(8,128)(2,1)S(1)} collective-permute-done((bf16[4,16,64,128]{3,2,1,0:T(8,128)(2,1)}, bf16[4,16,64,128]{3,2,1,0:T(8,128)(2,1)S(1)}, u32[]{:S(2)}, u32[]{:S(2)}) %collective-permute-start) | collective-permute-done | bytes 1048608 | tf_op jit(solution)/shard_map/while/body/eval_jaxpr/ppermute | solution.py:20
  486.7 15.3 %collective-permute-done = bf16[4,16,64,128]{3,2,1,0:T(8,128)(2,1)S(1)} collective-permute-done((bf16[4,16,64,128]{3,2,1,0:T(8,128)(2,1)}, bf16[4,16,64,128]{3,2,1,0:T(8,128)(2,1)S(1)}, u32[]{:S(2)}, u32[]{:S(2)}) %collective-permute-start) | collective-permute-done | bytes 1048608 | tf_op jit(solution)/shard_map/while/body/eval_jaxpr/ppermute | solution.py:20
  506.0 15.3 %collective-permute-done = bf16[4,16,64,128]{3,2,1,0:T(8,128)(2,1)S(1)} collective-permute-done((bf16[4,16,64,128]{3,2,1,0:T(8,128)(2,1)}, bf16[4,16,64,128]{3,2,1,0:T(8,128)(2,1)S(1)}, u32[]{:S(2)}, u32[]{:S(2)}) %collective-permute-start) | collective-permute-done | bytes 1048608 | tf_op jit(solution)/shard_map/while/body/eval_jaxpr/ppermute | solution.py:20
  525.2 15.3 %collective-permute-done = bf16[4,16,64,128]{3,2,1,0:T(8,128)(2,1)S(1)} collective-permute-done((bf16[4,16,64,128]{3,2,1,0:T(8,128)(2,1)}, bf16[4,16,64,128]{3,2,1,0:T(8,128)(2,1)S(1)}, u32[]{:S(2)}, u32[]{:S(2)}) %collective-permute-start) | collective-permute-done | bytes 1048608 | tf_op jit(solution)/shard_map/while/body/eval_jaxpr/ppermute | solution.py:20
  544.4 15.3 %collective-permute-done = bf16[4,16,64,128]{3,2,1,0:T(8,128)(2,1)S(1)} collective-permute-done((bf16[4,16,64,128]{3,2,1,0:T(8,128)(2,1)}, bf16[4,16,64,128]{3,2,1,0:T(8,128)(2,1)S(1)}, u32[]{:S(2)}, u32[]{:S(2)}) %collective-permute-start) | collective-permute-done | bytes 1048608 | tf_op jit(solution)/shard_map/while/body/eval_jaxpr/ppermute | solution.py:20
  563.7 15.3 %collective-permute-done = bf16[4,16,64,128]{3,2,1,0:T(8,128)(2,1)S(1)} collective-permute-done((bf16[4,16,64,128]{3,2,1,0:T(8,128)(2,1)}, bf16[4,16,64,128]{3,2,1,0:T(8,128)(2,1)S(1)}, u32[]{:S(2)}, u32[]{:S(2)}) %collective-permute-start) | collective-permute-done | bytes 1048608 | tf_op jit(solution)/shard_map/while/body/eval_jaxpr/ppermute | solution.py:20
  582.9 15.3 %collective-permute-done = bf16[4,16,64,128]{3,2,1,0:T(8,128)(2,1)S(1)} collective-permute-done((bf16[4,16,64,128]{3,2,1,0:T(8,128)(2,1)}, bf16[4,16,64,128]{3,2,1,0:T(8,128)(2,1)S(1)}, u32[]{:S(2)}, u32[]{:S(2)}) %collective-permute-start) | collective-permute-done | bytes 1048608 | tf_op jit(solution)/shard_map/while/body/eval_jaxpr/ppermute | solution.py:20
  602.1 15.3 %collective-permute-done = bf16[4,16,64,128]{3,2,1,0:T(8,128)(2,1)S(1)} collective-permute-done((bf16[4,16,64,128]{3,2,1,0:T(8,128)(2,1)}, bf16[4,16,64,128]{3,2,1,0:T(8,128)(2,1)S(1)}, u32[]{:S(2)}, u32[]{:S(2)}) %collective-permute-start) | collective-permute-done | bytes 1048608 | tf_op jit(solution)/shard_map/while/body/eval_jaxpr/ppermute | solution.py:20
  621.3 15.3 %collective-permute-done = bf16[4,16,64,128]{3,2,1,0:T(8,128)(2,1)S(1)} collective-permute-done((bf16[4,16,64,128]{3,2,1,0:T(8,128)(2,1)}, bf16[4,16,64,128]{3,2,1,0:T(8,128)(2,1)S(1)}, u32[]{:S(2)}, u32[]{:S(2)}) %collective-permute-start) | collective-permute-done | bytes 1048608 | tf_op jit(solution)/shard_map/while/body/eval_jaxpr/ppermute | solution.py:20
  639.7 5.5 fusion.52
  645.6 9.6 %fusion.28 = f32[256,4,16,64]{0,3,2,1:T(8,128)} fusion(bf16[256,4,16,64]{0,3,2,1:T(8,128)(2,1)S(1)} %bitcast.118, f32[4,16,64,256]{3,2,1,0:T(8,128)} %fusion.52, f32[4,16,256]{2,1,0:T(8,128)} %bitcast.129, f32[4,16,256]{2,1,0:T(8,128)S(1)} %copy_bitcast_fusion.1, f32[4,256,256]{2,1,0:T(8,128)S(1)} %fusion.47, pred[256,256]{1,0:T(8,128)(4,1)S(1)} %iota_compare_fusion, ...), kind=kOutput, calls=%fused_computation.40 | convolution fusion | flops 567279616 | bytes 11796736 | tf_op jit(solution)/shard_map/ghts,sghp->tghp/dot_general | solution.py:120
  655.2 5.7 copy.69
  664.7 4.9 psum.7
  669.6 5.2 multiply_convert_fusion
  (310 shorter events, 227.2 us)
Async XLA Ops:
  0.6 5.7 copy-start.7
  7.9 3.2 copy-start
  7.9 3.2 copy-start.8
  21.2 11.4 %collective-permute-start.1 = (bf16[2,256,512]{1,2,0:T(8,128)(2,1)S(1)}, bf16[2,256,512]{1,2,0:T(8,128)(2,1)S(1)}, u32[]{:S(2)}, u32[]{:S(2)}) collective-permute-start(bf16[2,256,512]{1,2,0:T(8,128)(2,1)S(1)} %get-tuple-element.441), channel_id=1, source_target_pairs={{0,2},{2,4},{4,6},{6,8},{8,10},{10,12},{12,14},{14,16},{16,18},{18... | collective-permute-start | bytes 1572872 | tf_op jit(solution)/shard_map/while/body/eval_jaxpr/ppermute | solution.py:20
  42.1 11.4 %collective-permute-start.1 = (bf16[2,256,512]{1,2,0:T(8,128)(2,1)S(1)}, bf16[2,256,512]{1,2,0:T(8,128)(2,1)S(1)}, u32[]{:S(2)}, u32[]{:S(2)}) collective-permute-start(bf16[2,256,512]{1,2,0:T(8,128)(2,1)S(1)} %get-tuple-element.441), channel_id=1, source_target_pairs={{0,2},{2,4},{4,6},{6,8},{8,10},{10,12},{12,14},{14,16},{16,18},{18... | collective-permute-start | bytes 1572872 | tf_op jit(solution)/shard_map/while/body/eval_jaxpr/ppermute | solution.py:20
  63.0 11.4 %collective-permute-start.1 = (bf16[2,256,512]{1,2,0:T(8,128)(2,1)S(1)}, bf16[2,256,512]{1,2,0:T(8,128)(2,1)S(1)}, u32[]{:S(2)}, u32[]{:S(2)}) collective-permute-start(bf16[2,256,512]{1,2,0:T(8,128)(2,1)S(1)} %get-tuple-element.441), channel_id=1, source_target_pairs={{0,2},{2,4},{4,6},{6,8},{8,10},{10,12},{12,14},{14,16},{16,18},{18... | collective-permute-start | bytes 1572872 | tf_op jit(solution)/shard_map/while/body/eval_jaxpr/ppermute | solution.py:20
  83.8 11.4 %collective-permute-start.1 = (bf16[2,256,512]{1,2,0:T(8,128)(2,1)S(1)}, bf16[2,256,512]{1,2,0:T(8,128)(2,1)S(1)}, u32[]{:S(2)}, u32[]{:S(2)}) collective-permute-start(bf16[2,256,512]{1,2,0:T(8,128)(2,1)S(1)} %get-tuple-element.441), channel_id=1, source_target_pairs={{0,2},{2,4},{4,6},{6,8},{8,10},{10,12},{12,14},{14,16},{16,18},{18... | collective-permute-start | bytes 1572872 | tf_op jit(solution)/shard_map/while/body/eval_jaxpr/ppermute | solution.py:20
  96.8 2.2 copy-start.4
  104.7 11.4 %collective-permute-start.1 = (bf16[2,256,512]{1,2,0:T(8,128)(2,1)S(1)}, bf16[2,256,512]{1,2,0:T(8,128)(2,1)S(1)}, u32[]{:S(2)}, u32[]{:S(2)}) collective-permute-start(bf16[2,256,512]{1,2,0:T(8,128)(2,1)S(1)} %get-tuple-element.441), channel_id=1, source_target_pairs={{0,2},{2,4},{4,6},{6,8},{8,10},{10,12},{12,14},{14,16},{16,18},{18... | collective-permute-start | bytes 1572872 | tf_op jit(solution)/shard_map/while/body/eval_jaxpr/ppermute | solution.py:20
  117.6 2.2 copy-start.4
  125.5 11.4 %collective-permute-start.1 = (bf16[2,256,512]{1,2,0:T(8,128)(2,1)S(1)}, bf16[2,256,512]{1,2,0:T(8,128)(2,1)S(1)}, u32[]{:S(2)}, u32[]{:S(2)}) collective-permute-start(bf16[2,256,512]{1,2,0:T(8,128)(2,1)S(1)} %get-tuple-element.441), channel_id=1, source_target_pairs={{0,2},{2,4},{4,6},{6,8},{8,10},{10,12},{12,14},{14,16},{16,18},{18... | collective-permute-start | bytes 1572872 | tf_op jit(solution)/shard_map/while/body/eval_jaxpr/ppermute | solution.py:20
  146.4 11.4 %collective-permute-start.1 = (bf16[2,256,512]{1,2,0:T(8,128)(2,1)S(1)}, bf16[2,256,512]{1,2,0:T(8,128)(2,1)S(1)}, u32[]{:S(2)}, u32[]{:S(2)}) collective-permute-start(bf16[2,256,512]{1,2,0:T(8,128)(2,1)S(1)} %get-tuple-element.441), channel_id=1, source_target_pairs={{0,2},{2,4},{4,6},{6,8},{8,10},{10,12},{12,14},{14,16},{16,18},{18... | collective-permute-start | bytes 1572872 | tf_op jit(solution)/shard_map/while/body/eval_jaxpr/ppermute | solution.py:20
  167.2 11.4 %collective-permute-start.1 = (bf16[2,256,512]{1,2,0:T(8,128)(2,1)S(1)}, bf16[2,256,512]{1,2,0:T(8,128)(2,1)S(1)}, u32[]{:S(2)}, u32[]{:S(2)}) collective-permute-start(bf16[2,256,512]{1,2,0:T(8,128)(2,1)S(1)} %get-tuple-element.441), channel_id=1, source_target_pairs={{0,2},{2,4},{4,6},{6,8},{8,10},{10,12},{12,14},{14,16},{16,18},{18... | collective-permute-start | bytes 1572872 | tf_op jit(solution)/shard_map/while/body/eval_jaxpr/ppermute | solution.py:20
  180.2 2.2 copy-start.4
  188.1 11.4 %collective-permute-start.1 = (bf16[2,256,512]{1,2,0:T(8,128)(2,1)S(1)}, bf16[2,256,512]{1,2,0:T(8,128)(2,1)S(1)}, u32[]{:S(2)}, u32[]{:S(2)}) collective-permute-start(bf16[2,256,512]{1,2,0:T(8,128)(2,1)S(1)} %get-tuple-element.441), channel_id=1, source_target_pairs={{0,2},{2,4},{4,6},{6,8},{8,10},{10,12},{12,14},{14,16},{16,18},{18... | collective-permute-start | bytes 1572872 | tf_op jit(solution)/shard_map/while/body/eval_jaxpr/ppermute | solution.py:20
  208.9 11.4 %collective-permute-start.1 = (bf16[2,256,512]{1,2,0:T(8,128)(2,1)S(1)}, bf16[2,256,512]{1,2,0:T(8,128)(2,1)S(1)}, u32[]{:S(2)}, u32[]{:S(2)}) collective-permute-start(bf16[2,256,512]{1,2,0:T(8,128)(2,1)S(1)} %get-tuple-element.441), channel_id=1, source_target_pairs={{0,2},{2,4},{4,6},{6,8},{8,10},{10,12},{12,14},{14,16},{16,18},{18... | collective-permute-start | bytes 1572872 | tf_op jit(solution)/shard_map/while/body/eval_jaxpr/ppermute | solution.py:20
  229.8 11.4 %collective-permute-start.1 = (bf16[2,256,512]{1,2,0:T(8,128)(2,1)S(1)}, bf16[2,256,512]{1,2,0:T(8,128)(2,1)S(1)}, u32[]{:S(2)}, u32[]{:S(2)}) collective-permute-start(bf16[2,256,512]{1,2,0:T(8,128)(2,1)S(1)} %get-tuple-element.441), channel_id=1, source_target_pairs={{0,2},{2,4},{4,6},{6,8},{8,10},{10,12},{12,14},{14,16},{16,18},{18... | collective-permute-start | bytes 1572872 | tf_op jit(solution)/shard_map/while/body/eval_jaxpr/ppermute | solution.py:20
  242.8 2.2 copy-start.4
  250.7 11.4 %collective-permute-start.1 = (bf16[2,256,512]{1,2,0:T(8,128)(2,1)S(1)}, bf16[2,256,512]{1,2,0:T(8,128)(2,1)S(1)}, u32[]{:S(2)}, u32[]{:S(2)}) collective-permute-start(bf16[2,256,512]{1,2,0:T(8,128)(2,1)S(1)} %get-tuple-element.441), channel_id=1, source_target_pairs={{0,2},{2,4},{4,6},{6,8},{8,10},{10,12},{12,14},{14,16},{16,18},{18... | collective-permute-start | bytes 1572872 | tf_op jit(solution)/shard_map/while/body/eval_jaxpr/ppermute | solution.py:20
  263.6 2.2 copy-start.4
  271.5 11.4 %collective-permute-start.1 = (bf16[2,256,512]{1,2,0:T(8,128)(2,1)S(1)}, bf16[2,256,512]{1,2,0:T(8,128)(2,1)S(1)}, u32[]{:S(2)}, u32[]{:S(2)}) collective-permute-start(bf16[2,256,512]{1,2,0:T(8,128)(2,1)S(1)} %get-tuple-element.441), channel_id=1, source_target_pairs={{0,2},{2,4},{4,6},{6,8},{8,10},{10,12},{12,14},{14,16},{16,18},{18... | collective-permute-start | bytes 1572872 | tf_op jit(solution)/shard_map/while/body/eval_jaxpr/ppermute | solution.py:20
  292.4 11.4 %collective-permute-start.1 = (bf16[2,256,512]{1,2,0:T(8,128)(2,1)S(1)}, bf16[2,256,512]{1,2,0:T(8,128)(2,1)S(1)}, u32[]{:S(2)}, u32[]{:S(2)}) collective-permute-start(bf16[2,256,512]{1,2,0:T(8,128)(2,1)S(1)} %get-tuple-element.441), channel_id=1, source_target_pairs={{0,2},{2,4},{4,6},{6,8},{8,10},{10,12},{12,14},{14,16},{16,18},{18... | collective-permute-start | bytes 1572872 | tf_op jit(solution)/shard_map/while/body/eval_jaxpr/ppermute | solution.py:20
  305.3 2.2 copy-start.4
  313.2 11.4 %collective-permute-start.1 = (bf16[2,256,512]{1,2,0:T(8,128)(2,1)S(1)}, bf16[2,256,512]{1,2,0:T(8,128)(2,1)S(1)}, u32[]{:S(2)}, u32[]{:S(2)}) collective-permute-start(bf16[2,256,512]{1,2,0:T(8,128)(2,1)S(1)} %get-tuple-element.441), channel_id=1, source_target_pairs={{0,2},{2,4},{4,6},{6,8},{8,10},{10,12},{12,14},{14,16},{16,18},{18... | collective-permute-start | bytes 1572872 | tf_op jit(solution)/shard_map/while/body/eval_jaxpr/ppermute | solution.py:20
  337.1 3.7 copy-start.13
  337.1 3.7 copy-start.6
  338.5 4.8 copy-start.9
  338.5 4.9 copy-start.11
  338.5 7.7 %copy-start.12 = (f32[64,256]{1,0:T(8,128)S(1)}, f32[64,256]{1,0:T(8,128)}, u32[]{:S(2)}) copy-start(f32[64,256]{1,0:T(8,128)} %param.22) | copy-start | bytes 196612
  350.2 17.2 %collective-permute-start = (bf16[4,16,64,128]{3,2,1,0:T(8,128)(2,1)}, bf16[4,16,64,128]{3,2,1,0:T(8,128)(2,1)S(1)}, u32[]{:S(2)}, u32[]{:S(2)}) collective-permute-start(bf16[4,16,64,128]{3,2,1,0:T(8,128)(2,1)} %get-tuple-element.472), channel_id=1, source_target_pairs={{0,2},{2,4},{4,6},{6,8},{8,10},{10,12},{12,14},{14,16},{16,18},{18... | collective-permute-start | bytes 3145736 | tf_op jit(solution)/shard_map/while/body/eval_jaxpr/ppermute | solution.py:20
  369.5 17.2 %collective-permute-start = (bf16[4,16,64,128]{3,2,1,0:T(8,128)(2,1)}, bf16[4,16,64,128]{3,2,1,0:T(8,128)(2,1)S(1)}, u32[]{:S(2)}, u32[]{:S(2)}) collective-permute-start(bf16[4,16,64,128]{3,2,1,0:T(8,128)(2,1)} %get-tuple-element.472), channel_id=1, source_target_pairs={{0,2},{2,4},{4,6},{6,8},{8,10},{10,12},{12,14},{14,16},{16,18},{18... | collective-permute-start | bytes 3145736 | tf_op jit(solution)/shard_map/while/body/eval_jaxpr/ppermute | solution.py:20
  388.7 17.2 %collective-permute-start = (bf16[4,16,64,128]{3,2,1,0:T(8,128)(2,1)}, bf16[4,16,64,128]{3,2,1,0:T(8,128)(2,1)S(1)}, u32[]{:S(2)}, u32[]{:S(2)}) collective-permute-start(bf16[4,16,64,128]{3,2,1,0:T(8,128)(2,1)} %get-tuple-element.472), channel_id=1, source_target_pairs={{0,2},{2,4},{4,6},{6,8},{8,10},{10,12},{12,14},{14,16},{16,18},{18... | collective-permute-start | bytes 3145736 | tf_op jit(solution)/shard_map/while/body/eval_jaxpr/ppermute | solution.py:20
  407.9 17.2 %collective-permute-start = (bf16[4,16,64,128]{3,2,1,0:T(8,128)(2,1)}, bf16[4,16,64,128]{3,2,1,0:T(8,128)(2,1)S(1)}, u32[]{:S(2)}, u32[]{:S(2)}) collective-permute-start(bf16[4,16,64,128]{3,2,1,0:T(8,128)(2,1)} %get-tuple-element.472), channel_id=1, source_target_pairs={{0,2},{2,4},{4,6},{6,8},{8,10},{10,12},{12,14},{14,16},{16,18},{18... | collective-permute-start | bytes 3145736 | tf_op jit(solution)/shard_map/while/body/eval_jaxpr/ppermute | solution.py:20
  427.2 17.2 %collective-permute-start = (bf16[4,16,64,128]{3,2,1,0:T(8,128)(2,1)}, bf16[4,16,64,128]{3,2,1,0:T(8,128)(2,1)S(1)}, u32[]{:S(2)}, u32[]{:S(2)}) collective-permute-start(bf16[4,16,64,128]{3,2,1,0:T(8,128)(2,1)} %get-tuple-element.472), channel_id=1, source_target_pairs={{0,2},{2,4},{4,6},{6,8},{8,10},{10,12},{12,14},{14,16},{16,18},{18... | collective-permute-start | bytes 3145736 | tf_op jit(solution)/shard_map/while/body/eval_jaxpr/ppermute | solution.py:20
  446.4 17.2 %collective-permute-start = (bf16[4,16,64,128]{3,2,1,0:T(8,128)(2,1)}, bf16[4,16,64,128]{3,2,1,0:T(8,128)(2,1)S(1)}, u32[]{:S(2)}, u32[]{:S(2)}) collective-permute-start(bf16[4,16,64,128]{3,2,1,0:T(8,128)(2,1)} %get-tuple-element.472), channel_id=1, source_target_pairs={{0,2},{2,4},{4,6},{6,8},{8,10},{10,12},{12,14},{14,16},{16,18},{18... | collective-permute-start | bytes 3145736 | tf_op jit(solution)/shard_map/while/body/eval_jaxpr/ppermute | solution.py:20
  465.6 17.2 %collective-permute-start = (bf16[4,16,64,128]{3,2,1,0:T(8,128)(2,1)}, bf16[4,16,64,128]{3,2,1,0:T(8,128)(2,1)S(1)}, u32[]{:S(2)}, u32[]{:S(2)}) collective-permute-start(bf16[4,16,64,128]{3,2,1,0:T(8,128)(2,1)} %get-tuple-element.472), channel_id=1, source_target_pairs={{0,2},{2,4},{4,6},{6,8},{8,10},{10,12},{12,14},{14,16},{16,18},{18... | collective-permute-start | bytes 3145736 | tf_op jit(solution)/shard_map/while/body/eval_jaxpr/ppermute | solution.py:20
  484.8 17.2 %collective-permute-start = (bf16[4,16,64,128]{3,2,1,0:T(8,128)(2,1)}, bf16[4,16,64,128]{3,2,1,0:T(8,128)(2,1)S(1)}, u32[]{:S(2)}, u32[]{:S(2)}) collective-permute-start(bf16[4,16,64,128]{3,2,1,0:T(8,128)(2,1)} %get-tuple-element.472), channel_id=1, source_target_pairs={{0,2},{2,4},{4,6},{6,8},{8,10},{10,12},{12,14},{14,16},{16,18},{18... | collective-permute-start | bytes 3145736 | tf_op jit(solution)/shard_map/while/body/eval_jaxpr/ppermute | solution.py:20
  504.1 17.2 %collective-permute-start = (bf16[4,16,64,128]{3,2,1,0:T(8,128)(2,1)}, bf16[4,16,64,128]{3,2,1,0:T(8,128)(2,1)S(1)}, u32[]{:S(2)}, u32[]{:S(2)}) collective-permute-start(bf16[4,16,64,128]{3,2,1,0:T(8,128)(2,1)} %get-tuple-element.472), channel_id=1, source_target_pairs={{0,2},{2,4},{4,6},{6,8},{8,10},{10,12},{12,14},{14,16},{16,18},{18... | collective-permute-start | bytes 3145736 | tf_op jit(solution)/shard_map/while/body/eval_jaxpr/ppermute | solution.py:20
  523.3 17.2 %collective-permute-start = (bf16[4,16,64,128]{3,2,1,0:T(8,128)(2,1)}, bf16[4,16,64,128]{3,2,1,0:T(8,128)(2,1)S(1)}, u32[]{:S(2)}, u32[]{:S(2)}) collective-permute-start(bf16[4,16,64,128]{3,2,1,0:T(8,128)(2,1)} %get-tuple-element.472), channel_id=1, source_target_pairs={{0,2},{2,4},{4,6},{6,8},{8,10},{10,12},{12,14},{14,16},{16,18},{18... | collective-permute-start | bytes 3145736 | tf_op jit(solution)/shard_map/while/body/eval_jaxpr/ppermute | solution.py:20
  542.5 17.2 %collective-permute-start = (bf16[4,16,64,128]{3,2,1,0:T(8,128)(2,1)}, bf16[4,16,64,128]{3,2,1,0:T(8,128)(2,1)S(1)}, u32[]{:S(2)}, u32[]{:S(2)}) collective-permute-start(bf16[4,16,64,128]{3,2,1,0:T(8,128)(2,1)} %get-tuple-element.472), channel_id=1, source_target_pairs={{0,2},{2,4},{4,6},{6,8},{8,10},{10,12},{12,14},{14,16},{16,18},{18... | collective-permute-start | bytes 3145736 | tf_op jit(solution)/shard_map/while/body/eval_jaxpr/ppermute | solution.py:20
  561.7 17.2 %collective-permute-start = (bf16[4,16,64,128]{3,2,1,0:T(8,128)(2,1)}, bf16[4,16,64,128]{3,2,1,0:T(8,128)(2,1)S(1)}, u32[]{:S(2)}, u32[]{:S(2)}) collective-permute-start(bf16[4,16,64,128]{3,2,1,0:T(8,128)(2,1)} %get-tuple-element.472), channel_id=1, source_target_pairs={{0,2},{2,4},{4,6},{6,8},{8,10},{10,12},{12,14},{14,16},{16,18},{18... | collective-permute-start | bytes 3145736 | tf_op jit(solution)/shard_map/while/body/eval_jaxpr/ppermute | solution.py:20
  581.0 17.2 %collective-permute-start = (bf16[4,16,64,128]{3,2,1,0:T(8,128)(2,1)}, bf16[4,16,64,128]{3,2,1,0:T(8,128)(2,1)S(1)}, u32[]{:S(2)}, u32[]{:S(2)}) collective-permute-start(bf16[4,16,64,128]{3,2,1,0:T(8,128)(2,1)} %get-tuple-element.472), channel_id=1, source_target_pairs={{0,2},{2,4},{4,6},{6,8},{8,10},{10,12},{12,14},{14,16},{16,18},{18... | collective-permute-start | bytes 3145736 | tf_op jit(solution)/shard_map/while/body/eval_jaxpr/ppermute | solution.py:20
  600.2 17.2 %collective-permute-start = (bf16[4,16,64,128]{3,2,1,0:T(8,128)(2,1)}, bf16[4,16,64,128]{3,2,1,0:T(8,128)(2,1)S(1)}, u32[]{:S(2)}, u32[]{:S(2)}) collective-permute-start(bf16[4,16,64,128]{3,2,1,0:T(8,128)(2,1)} %get-tuple-element.472), channel_id=1, source_target_pairs={{0,2},{2,4},{4,6},{6,8},{8,10},{10,12},{12,14},{14,16},{16,18},{18... | collective-permute-start | bytes 3145736 | tf_op jit(solution)/shard_map/while/body/eval_jaxpr/ppermute | solution.py:20
  619.4 17.2 %collective-permute-start = (bf16[4,16,64,128]{3,2,1,0:T(8,128)(2,1)}, bf16[4,16,64,128]{3,2,1,0:T(8,128)(2,1)S(1)}, u32[]{:S(2)}, u32[]{:S(2)}) collective-permute-start(bf16[4,16,64,128]{3,2,1,0:T(8,128)(2,1)} %get-tuple-element.472), channel_id=1, source_target_pairs={{0,2},{2,4},{4,6},{6,8},{8,10},{10,12},{12,14},{14,16},{16,18},{18... | collective-permute-start | bytes 3145736 | tf_op jit(solution)/shard_map/while/body/eval_jaxpr/ppermute | solution.py:20
  639.7 5.5 copy-start.10
  639.7 5.8 copy-start.14
  639.7 5.9 copy-start.3
  655.2 5.8 copy-start.2
  (25 other events, 50.6 us)
where the time goes:
time: 677 us; the launch traced here: 675 us
  waiting for transfers between devices  370 us (55%)
  matrix products  106 us (16%)
  other arithmetic  81.5 us (12%)
  starting transfers between devices  57.3 us (8%)
  local copies, waits for them, and re-layouts  53 us (8%)
    ppermute x30, waiting for transfers between devices, passed_along(): return lax.ppermute(block, axis, route)  370 us
    dot_general x16, matrix products, sub_step(): jnp.einsum('wlhc,cwm->wlhm', weights.astype(jnp.bfloat16), value_portion,...  63.1 us
    ppermute x30, starting transfers between devices, passed_along(): return lax.ppermute(block, axis, route)  57.3 us
    reduce_sum x16, other arithmetic, sub_step(): run_sum = run_sum * correction_factor + jnp.sum(weights, axis=-1)  34.1 us
    add x15, other arithmetic, relay_step(): return (received, block_decay[..., None, None] * received + local_state)  30.2 us
    while x90, local copies, waits for them, and re-layouts  29.3 us
    dot_general x16, matrix products, sub_step(): jnp.einsum('faqo,bao->aqfb', query_head_rows, key_portion, preferred_elem...  24 us
    unnamed x32, local copies, waits for them, and re-layouts  14.4 us
  transfers between devices with their start and end apart: 30, of which 30 were waited for; matrix products, arithmetic and copies ran while one was open for 0% of the time, Pallas kernels for 0%

commit v1 on v0

v1 whole, which is shorter than its diff:
```python
import functools
import math

import jax
import jax.numpy as jnp
from jax import lax
from jax.experimental import pallas as pl
from jax.experimental.pallas import tpu as pltpu
from jax.sharding import PartitionSpec as P

HEAD_WIDTH = 128
STATE_HEADS = 128
P_SIZE = 64
N = 128
CHUNK = 1024
HEADS_STEP = 4
VMEM_LIMIT = 48 * 1024 * 1024

causal_score = -1e30


def passed_along(block, axis, distance):
    devices = range(lax.axis_size(axis))
    route = [(i - distance, i) for i in devices if i - distance in devices]
    return lax.ppermute(block, axis, route)


def swapped(block, axis):
    return lax.ppermute(block, axis, [(i, i ^ 1) for i in range(lax.axis_size(axis))])


def attend_kernel(chunk, *refs):
    kv_ref, q_ref = refs[:2]
    o_ref, m_scr, acc_scr = refs[-3:]
    rows = q_ref.shape[0]
    heads = q_ref.shape[1] // HEAD_WIDTH
    factor = HEAD_WIDTH ** (-0.5) * math.log2(math.e)
    q_start = lax.axis_index("ctx") * rows
    last = q_start // chunk

    def sweep(c, first):
        start = pl.multiple_of(c * chunk, chunk)
        keys = kv_ref[pl.ds(start, chunk), :HEAD_WIDTH]
        values = kv_ref[pl.ds(start, chunk), HEAD_WIDTH:]
        values = jnp.concatenate([values, jnp.ones_like(values)], axis=1)
        if first:
            gap = lax.broadcasted_iota(jnp.int32, (rows, chunk), 0) - lax.broadcasted_iota(
                jnp.int32, (rows, chunk), 1
            )
            valid = gap >= start - q_start

        @pl.loop(0, heads // HEADS_STEP)
        def _(outer):
            for inner in range(HEADS_STEP):
                h = outer * HEADS_STEP + inner
                q = q_ref[:, pl.ds(pl.multiple_of(h * HEAD_WIDTH, HEAD_WIDTH), HEAD_WIDTH)]
                s = lax.dot_general(
                    q, keys, (((1,), (1,)), ((), ())), preferred_element_type=jnp.float32
                )
                if first:
                    s = jnp.where(valid, s, causal_score)
                top = jnp.max(s, axis=1, keepdims=True)
                if first:
                    p = jnp.exp2((s - top) * factor)
                    acc_scr[h] = jnp.dot(
                        p.astype(jnp.bfloat16), values, preferred_element_type=jnp.float32
                    )
                    m_scr[h] = jnp.broadcast_to(top, (rows, HEAD_WIDTH))
                else:
                    old = m_scr[h]
                    new = jnp.maximum(old, top)
                    p = jnp.exp2((s - new[:, :1]) * factor)
                    r = jnp.dot(p.astype(jnp.bfloat16), values, preferred_element_type=jnp.float32)
                    a = jnp.exp2((old - new) * factor)
                    acc_scr[h, :, :HEAD_WIDTH] = acc_scr[h, :, :HEAD_WIDTH] * a + r[:, :HEAD_WIDTH]
                    acc_scr[h, :, HEAD_WIDTH:] = acc_scr[h, :, HEAD_WIDTH:] * a + r[:, HEAD_WIDTH:]
                    m_scr[h] = new

    sweep(last, True)

    @pl.loop(0, last)
    def _(c):
        sweep(c, False)

    for h in range(heads):
        o_ref[:, h * HEAD_WIDTH : (h + 1) * HEAD_WIDTH] = (
            acc_scr[h, :, :HEAD_WIDTH] / acc_scr[h, :, HEAD_WIDTH:]
        ).astype(o_ref.dtype)


def attend(kv, queries, so_far, head, kv_heads):
    rows, width = queries.shape
    cols = width // kv_heads
    keys = kv.shape[0]
    chunk = CHUNK if keys % CHUNK == 0 and CHUNK % rows == 0 else rows
    q_heads = cols // HEAD_WIDTH
    in_specs = [
        pl.BlockSpec((keys, 2 * HEAD_WIDTH), lambda i: (0, 0)),
        pl.BlockSpec((rows, cols), lambda i: (0, head)),
    ]
    operands = [kv, queries]
    aliases = {}
    if so_far is not None:
        in_specs.append(pl.BlockSpec(memory_space=pl.ANY))
        operands.append(so_far)
        aliases = {2: 0}
    return pl.pallas_call(
        functools.partial(attend_kernel, chunk),
        grid=(1,),
        out_shape=jax.ShapeDtypeStruct((rows, width), jnp.bfloat16),
        in_specs=in_specs,
        out_specs=pl.BlockSpec((rows, cols), lambda i: (0, head)),
        scratch_shapes=[
            pltpu.VMEM((q_heads, rows, HEAD_WIDTH), jnp.float32),
            pltpu.VMEM((q_heads, rows, 2 * HEAD_WIDTH), jnp.float32),
        ],
        input_output_aliases=aliases,
        compiler_params=pltpu.CompilerParams(vmem_limit_bytes=VMEM_LIMIT),
        cost_estimate=pl.CostEstimate(
            flops=8 * rows * keys * cols, bytes_accessed=4 * keys * HEAD_WIDTH, transcendentals=0
        ),
        name="attend",
    )(*operands)


def pair_select(rows, first, second):
    lane = lax.broadcasted_iota(jnp.int32, (rows, 2 * P_SIZE), 1)
    return jnp.where(lane < P_SIZE, first, second)


def state_kernel(x_ref, b_ref, w_ref, s_ref):
    rows = x_ref.shape[0]
    maps = b_ref[...]
    for pair in range(x_ref.shape[1] // (2 * P_SIZE)):
        lanes = slice(pair * 2 * P_SIZE, (pair + 1) * 2 * P_SIZE)
        scale = pair_select(
            rows, w_ref[0, :, 2 * pair : 2 * pair + 1], w_ref[0, :, 2 * pair + 1 : 2 * pair + 2]
        )
        weighted = (x_ref[:, lanes].astype(jnp.float32) * scale).astype(jnp.bfloat16)
        s_ref[lanes, :] = lax.dot_general(
            weighted, maps, (((0,), (0,)), ((), ())), preferred_element_type=jnp.float32
        )


def inner_kernel(x_ref, b_ref, c_ref, ccol_ref, crow_ref, step_ref, skip_ref, y_ref):
    rows = x_ref.shape[0]
    gram = lax.dot_general(
        c_ref[...], b_ref[...], (((1,), (1,)), ((), ())), preferred_element_type=jnp.float32
    )
    causal = lax.broadcasted_iota(jnp.int32, (rows, rows), 0) >= lax.broadcasted_iota(
        jnp.int32, (rows, rows), 1
    )
    gram = jnp.where(causal, gram, 0.0)
    for pair in range(x_ref.shape[1] // (2 * P_SIZE)):
        lanes = slice(pair * 2 * P_SIZE, (pair + 1) * 2 * P_SIZE)
        x = x_ref[:, lanes]
        parts = []
        for h in (2 * pair, 2 * pair + 1):
            spread = jnp.minimum(ccol_ref[0, :, h : h + 1] - crow_ref[0, h : h + 1, :], 0.0)
            mixing = gram * jnp.exp(spread) * step_ref[0, h : h + 1, :]
            parts.append(
                jnp.dot(mixing.astype(jnp.bfloat16), x, preferred_element_type=jnp.float32)
            )
        direct = skip_ref[:, lanes] * x.astype(jnp.float32)
        y_ref[:, lanes] = pair_select(rows, parts[0], parts[1]) + direct


def gate_kernel(y_ref, s_ref, c_ref, e_ref, gate_ref, g_ref, sq_ref):
    rows = y_ref.shape[0]
    carried = lax.dot_general(
        c_ref[...], s_ref[...], (((1,), (1,)), ((), ())), preferred_element_type=jnp.float32
    )
    total = jnp.zeros((rows, 2 * P_SIZE), jnp.float32)
    for pair in range(y_ref.shape[1] // (2 * P_SIZE)):
        lanes = slice(pair * 2 * P_SIZE, (pair + 1) * 2 * P_SIZE)
        grow = pair_select(
            rows, e_ref[0, :, 2 * pair : 2 * pair + 1], e_ref[0, :, 2 * pair + 1 : 2 * pair + 2]
        )
        out = y_ref[:, lanes] + carried[:, lanes] * grow
        v = gate_ref[:, lanes].astype(jnp.float32)
        gated = out * (v / (1.0 + jnp.exp(-v)))
        g_ref[:, lanes] = gated
        total += gated * gated
    square = jnp.sum(total, axis=1, keepdims=True)

    @pl.when(pl.program_id(0) == 0)
    def _():
        sq_ref[...] = square

    @pl.when(pl.program_id(0) > 0)
    def _():
        sq_ref[...] += square


def norm_kernel(count, g_ref, sq_ref, gain_ref, o_ref):
    scaling = lax.rsqrt(sq_ref[...] / count + 1e-05)
    o_ref[...] = (g_ref[...] * scaling * gain_ref[...].astype(jnp.float32)).astype(o_ref.dtype)


def incoming_state(local_state, ends):
    count = lax.axis_size("ctx")
    position = lax.axis_index("ctx")
    heads = local_state.shape[0]
    half = heads // 2
    core = position % 2
    pair = position // 2
    pairs = count // 2
    all_ends = lax.all_gather(ends, "ctx")
    low = core == 0
    bf = jnp.bfloat16

    sent = jnp.where(low, local_state[half:], local_state[:half]).astype(bf)
    mine = jnp.where(low, local_state[:half], local_state[half:])
    theirs = swapped(sent, "ctx").astype(jnp.float32)
    ends_half = jnp.where(low, all_ends[:, :half], all_ends[:, half:])
    pair_ends = ends_half.reshape(pairs, 2, half)
    first = jnp.where(low, mine, theirs)
    second = jnp.where(low, theirs, mine)
    own = lax.dynamic_index_in_dim(pair_ends, pair, 0, keepdims=False)
    pair_logs = pair_ends[:, 0] + pair_ends[:, 1]
    index = jnp.arange(pairs)[:, None]

    def window(last, width):
        inside = (index > last - width) & (index <= last)
        return jnp.exp(jnp.sum(jnp.where(inside, pair_logs, 0.0), axis=0))[:, None, None]

    total = jnp.exp(own[1])[:, None, None] * first + second
    width = 1
    while 2 * width < pairs:
        before = passed_along(total.astype(bf), "ctx", 2 * width).astype(jnp.float32)
        total = total + window(pair, width) * before
        width *= 2
    packed = total.astype(bf)
    near = passed_along(packed, "ctx", 2).astype(jnp.float32)
    far = passed_along(packed, "ctx", 2 * (1 + width)).astype(jnp.float32)
    enter = near + window(pair - 1, width) * far
    enter_second = jnp.exp(own[0])[:, None, None] * enter + first
    for_me = jnp.where(low, enter, enter_second).astype(bf)
    for_them = jnp.where(low, enter_second, enter).astype(bf)
    got = swapped(for_them, "ctx")
    return jnp.where(
        low, jnp.concatenate([for_me, got], axis=0), jnp.concatenate([got, for_me], axis=0)
    )


def local(
    queries,
    key_rows,
    value_head_rows,
    ssm_input,
    gate_input,
    b_matrix,
    c_matrix,
    step_size,
    log_decay,
    skip_gain,
    norm_gain,
):
    rows = queries.shape[0]
    kv_heads = key_rows.shape[1] // HEAD_WIDTH
    gathered = []
    for g in range(kv_heads):
        cols = slice(g * HEAD_WIDTH, (g + 1) * HEAD_WIDTH)
        both = jnp.concatenate([key_rows[:, cols], value_head_rows[:, cols]], axis=1)
        gathered.append(lax.all_gather(both, "ctx", axis=0, tiled=True))

    heads = step_size.shape[0]
    groups = b_matrix.shape[1] // N
    per = heads // groups
    width = per * P_SIZE
    until = jnp.triu(jnp.ones((rows, rows), jnp.float32))
    cumul = jnp.dot(log_decay, until, precision=lax.Precision.HIGHEST)
    ends = cumul[:, -1]
    weight_end = jnp.exp(ends[:, None] - cumul) * step_size

    def by_group(a):
        return a.reshape(groups, per, rows)

    def columns(a):
        return by_group(a).transpose(0, 2, 1)

    params = pltpu.CompilerParams(vmem_limit_bytes=VMEM_LIMIT)
    wide = pl.BlockSpec((rows, width), lambda g: (0, g))
    narrow = pl.BlockSpec((rows, N), lambda g: (0, g))
    column = pl.BlockSpec((1, rows, per), lambda g: (g, 0, 0))
    row = pl.BlockSpec((1, per, rows), lambda g: (g, 0, 0))
    line = pl.BlockSpec((1, width), lambda g: (0, g))
    state = pl.BlockSpec((width, N), lambda g: (g, 0))

    local_state = pl.pallas_call(
        state_kernel,
        grid=(groups,),
        in_specs=[wide, narrow, column],
        out_specs=state,
        out_shape=jax.ShapeDtypeStruct((groups * width, N), jnp.float32),
        compiler_params=params,
        cost_estimate=pl.CostEstimate(
            flops=8 * rows * heads * P_SIZE * N, bytes_accessed=4 << 20, transcendentals=0
        ),
        name="local_state",
    )(ssm_input, b_matrix, columns(weight_end))

    entering = incoming_state(local_state.reshape(heads, P_SIZE, N), ends)

    inner = pl.pallas_call(
        inner_kernel,
        grid=(groups,),
        in_specs=[wide, narrow, narrow, column, row, row, line],
        out_specs=wide,
        out_shape=jax.ShapeDtypeStruct((rows, groups * width), jnp.float32),
        compiler_params=params,
        cost_estimate=pl.CostEstimate(
            flops=40 * rows * rows * heads * P_SIZE, bytes_accessed=6 << 20, transcendentals=0
        ),
        name="inner",
    )(
        ssm_input,
        b_matrix,
        c_matrix,
        columns(cumul),
        by_group(cumul),
        by_group(step_size),
        jnp.repeat(skip_gain, P_SIZE)[None, :],
    )

    attention_out = None
    for g in range(kv_heads):
        attention_out = attend(gathered[g], queries, attention_out, g, kv_heads)

    gated, square = pl.pallas_call(
        gate_kernel,
        grid=(groups,),
        in_specs=[wide, state, narrow, column, wide],
        out_specs=[wide, pl.BlockSpec((rows, 1), lambda g: (0, 0))],
        out_shape=[
            jax.ShapeDtypeStruct((rows, groups * width), jnp.float32),
            jax.ShapeDtypeStruct((rows, 1), jnp.float32),
        ],
        compiler_params=params,
        cost_estimate=pl.CostEstimate(
            flops=16 * rows * heads * P_SIZE * N, bytes_accessed=11 << 20, transcendentals=0
        ),
        name="gated",
    )(inner, entering.reshape(groups * width, N), c_matrix, columns(jnp.exp(cumul)), gate_input)
    square = lax.psum(square, "tp")
    mixer_out = pl.pallas_call(
        functools.partial(norm_kernel, STATE_HEADS * P_SIZE),
        grid=(groups,),
        in_specs=[wide, pl.BlockSpec((rows, 1), lambda g: (0, 0)), line],
        out_specs=wide,
        out_shape=jax.ShapeDtypeStruct((rows, groups * width), jnp.bfloat16),
        compiler_params=params,
        name="norm",
    )(gated, square, norm_gain[None, :])
    return (attention_out, mixer_out)


def solution(mesh):
    placed = (
        P("ctx", "tp"),
        P("ctx", "tp"),
        P("ctx", "tp"),
        P("ctx", "tp"),
        P("ctx", "tp"),
        P("ctx", "tp"),
        P("ctx", "tp"),
        P("tp", "ctx"),
        P("tp", "ctx"),
        P("tp"),
        P("tp"),
    )
    return jax.shard_map(
        local,
        mesh=mesh,
        in_specs=placed,
        out_specs=(P("ctx", "tp"), P("ctx", "tp")),
        check_vma=False,
    )
```

time: 677 us -> 231 us (0.34)
  waiting for transfers between devices: 370 us -> 49.5 us
  matrix products: 106 us -> 0.37 us
  Pallas kernels: 0 us -> 87.3 us
  other arithmetic: 81.5 us -> 7.95 us
  starting transfers between devices: 57.3 us -> 13.4 us
  local copies, waits for them, and re-layouts: 53 us -> 19.9 us
  blocking collectives: 4.93 us -> 33.9 us
  between operations: 0.94 us -> 14.8 us
    ppermute x30 -> x4, waiting for transfers between devices: 370 us -> 49.4 us  [passed_along(): return lax.ppermute(block, axis, route)]
    dot_general x36 -> x1, matrix products: 106 us -> 0.37 us  [local(): cumul = jnp.dot(log_decay, until, precision=lax.Precision.HIGHEST)]
    pallas_call x0 -> x8, Pallas kernels: none -> 87.3 us  [the longest x4 66.3 us: attend(): pl.pallas_call(functools.partial(attend_kernel, chunk), grid=(1,), out_sh...]
    ppermute x30 -> x4, starting transfers between devices: 57.3 us -> 13.1 us  [passed_along(): return lax.ppermute(block, axis, route)]
    reduce_sum x17 -> x1, other arithmetic: 37.8 us -> 0.09 us  [window(): jnp.sum(jnp.where(inside, pair_logs, 0.0), axis=0)]
    add x46 -> x2, other arithmetic: 30.5 us -> 0.01 us  [the longest x1 0.01 us: incoming_state(): pair_logs = pair_ends[:, 0] + pair_ends[:, 1]]
    while x90 -> x0, local copies, waits for them, and re-layouts: 29.3 us -> none
    unnamed x0 -> x1, blocking collectives: none -> 24.5 us
  transfers between devices with their start and end apart: 30 -> 10, of which waited for: 30 -> 3; matrix products, arithmetic and copies ran while one was open for 0% -> 6% of each run, Pallas kernels for 0% -> 31%
where the time goes in v1:
time: 231 us; the launch traced here: 227 us
  Pallas kernels  87.3 us (38%)
  waiting for transfers between devices  49.5 us (21%)
  blocking collectives  33.9 us (15%)
  local copies, waits for them, and re-layouts  19.9 us (9%)
  between operations  14.8 us (6%)
  starting transfers between devices  13.4 us (6%)
  other arithmetic  7.95 us (3%)
    pallas_call x4, Pallas kernels, attend(): pl.pallas_call(functools.partial(attend_kernel, chunk), grid=(1,), out_sh...  66.3 us
    ppermute x4, waiting for transfers between devices, passed_along(): return lax.ppermute(block, axis, route)  49.4 us
    unnamed x1, blocking collectives  24.5 us
    ppermute x4, starting transfers between devices, passed_along(): return lax.ppermute(block, axis, route)  13.1 us
    unnamed x45, local copies, waits for them, and re-layouts  12.5 us
    psum x1, blocking collectives, local(): square = lax.psum(square, 'tp')  9.36 us
    pallas_call x1, Pallas kernels, local(): pl.pallas_call(inner_kernel, grid=(groups,), in_specs=[wide, narrow, narr...  6.77 us
    pallas_call x1, Pallas kernels, local(): pl.pallas_call(gate_kernel, grid=(groups,), in_specs=[wide, state, narrow...  6.36 us
  transfers between devices with their start and end apart: 10, of which 3 were waited for; matrix products, arithmetic and copies ran while one was open for 6% of the time, Pallas kernels for 31%

profile of v1, /device:TPU:24, one launch (start us, length us, event | category | flops | bytes accessed | tf_op | source)
XLA Modules:
  0.0 227.1 jit_solution(7341535606459437428)
XLA Ops:
  7.2 1.8 fusion.10
  9.1 0.7 pad_maximum_fusion.3
  9.8 0.7 pad_maximum_fusion.2
  10.6 0.7 pad_maximum_fusion.1
  11.3 0.4 fusion.2
  11.7 0.2 slice_reduce_fusion
  11.9 0.6 bitcast_exponential_fusion
  12.5 0.2 copy.18
  12.8 1.6 copy-done.2
  14.4 5.5 %local_state.1 = f32[4096,128]{1,0:T(8,128)S(1)} custom-call(bf16[256,4096]{1,0:T(8,128)(2,1)S(1)} %copy-done.2, bf16[256,512]{1,0:T(8,128)(2,1)S(1)} %copy-done.5, f32[4,256,16]{2,1,0:T(8,128)S(1)} %bitcast.25), custom_call_target="tpu_custom_call" | custom-call | flops 1073741824 | bytes 4194304 | tf_op jit(solution)/shard_map/local_state/pallas_call | solution.py:290
  20.1 0.6 dynamic-slice
  21.3 0.2 dynamic-update-slice
  21.6 24.5 %all-reduce = f32[1024]{0:T(1024)S(1)} all-reduce(f32[1024]{0:T(1024)S(1)} %dynamic-update-slice), channel_id=2, replica_groups=mesh['ctx'=16,'tp'=2] {'ctx'}, use_global_device_ids=true, to_apply=%add | all-reduce | flops 1024 | bytes 8192
  46.3 0.6 exponential_bitcast_fusion
  46.8 0.1 slice_select_fusion
  47.0 0.3 fusion.9
  47.2 6.0 %collective-permute-start.1 = (bf16[32,64,128]{2,1,0:T(8,128)(2,1)S(1)}, bf16[32,64,128]{2,1,0:T(8,128)(2,1)S(1)}, u32[]{:S(2)}, u32[]{:S(2)}) collective-permute-start(bf16[32,64,128]{2,1,0:T(8,128)(2,1)S(1)} %fusion.9), channel_id=1, source_target_pairs={{0,4},{2,6},{4,8},{6,10},{8,12},{10,14},{12,16},{14,18},{16,20},{1... | collective-permute-start | bytes 1572872 | tf_op jit(solution)/shard_map/ppermute | solution.py:25
  53.4 12.1 %collective-permute-done.1 = bf16[32,64,128]{2,1,0:T(8,128)(2,1)S(1)} collective-permute-done((bf16[32,64,128]{2,1,0:T(8,128)(2,1)S(1)}, bf16[32,64,128]{2,1,0:T(8,128)(2,1)S(1)}, u32[]{:S(2)}, u32[]{:S(2)}) %collective-permute-start.1) | collective-permute-done | bytes 524320 | tf_op jit(solution)/shard_map/ppermute | solution.py:25
  65.4 0.4 fusion.1
  65.8 1.4 collective-permute-start.2
  67.3 19.0 %collective-permute-done.2 = bf16[32,64,128]{2,1,0:T(8,128)(2,1)S(1)} collective-permute-done((bf16[32,64,128]{2,1,0:T(8,128)(2,1)S(1)}, bf16[32,64,128]{2,1,0:T(8,128)(2,1)S(1)}, u32[]{:S(2)}, u32[]{:S(2)}) %collective-permute-start.2) | collective-permute-done | bytes 524320 | tf_op jit(solution)/shard_map/ppermute | solution.py:25
  86.3 1.3 add_convert_fusion
  87.6 4.3 %collective-permute-start.3 = (bf16[32,64,128]{2,1,0:T(8,128)(2,1)}, bf16[32,64,128]{2,1,0:T(8,128)(2,1)}, u32[]{:S(2)}, u32[]{:S(2)}) collective-permute-start(bf16[32,64,128]{2,1,0:T(8,128)(2,1)} %add_convert_fusion), channel_id=1, source_target_pairs={{0,4},{2,6},{4,8},{6,10},{8,12},{10,14},{12,16},{14,18},{16,20},{1... | collective-permute-start | bytes 1572872 | tf_op jit(solution)/shard_map/ppermute | solution.py:25
  91.9 1.3 collective-permute-start.4
  93.2 0.7 pad_maximum_fusion
  93.9 0.5 exp.52
  94.5 0.2 copy.19
  94.7 0.2 copy.17.ccol_ref
  94.9 1.5 broadcast_in_dim.45
  96.3 1.5 broadcast_in_dim_reshape.3.skip_ref
  97.8 0.8 broadcast_in_dim.50.gain_ref
  98.6 18.4 %collective-permute-done.3 = bf16[32,64,128]{2,1,0:T(8,128)(2,1)} collective-permute-done((bf16[32,64,128]{2,1,0:T(8,128)(2,1)}, bf16[32,64,128]{2,1,0:T(8,128)(2,1)}, u32[]{:S(2)}, u32[]{:S(2)}) %collective-permute-start.3) | collective-permute-done | bytes 524320 | tf_op jit(solution)/shard_map/ppermute | solution.py:25
  116.9 2.1 select_convert_fusion.1
  119.2 6.8 %inner.1.y_ref = f32[256,4096]{1,0:T(8,128)} custom-call(bf16[256,4096]{1,0:T(8,128)(2,1)S(1)} %copy-done.3, bf16[256,512]{1,0:T(8,128)(2,1)S(1)} %copy-done.5, bf16[256,512]{1,0:T(8,128)(2,1)S(1)} %copy-done.6, f32[4,256,16]{2,1,0:T(8,128)S(1)} %copy.17.ccol_ref, f32[4,16,256]{2,1,0:T(8,128)S(1)} %bitcast.28, f32[4,16,256]{2,1,0:T(8,128)S(1)} %bitcast.29, ...), custom_call_target="tpu_custom_call" | custom-call | flops 10737418240 | bytes 6291456 | tf_op jit(solution)/shard_map/inner/pallas_call | solution.py:305
  126.0 0.2 maximum_select_fusion
  126.1 1.4 copy-done.4
  127.6 6.4 %gated.1 = (f32[256,4096]{1,0:T(8,128)}, f32[256,1]{1,0:T(8,128)S(1)}) custom-call(f32[256,4096]{1,0:T(8,128)} %inner.1.y_ref, bf16[4096,128]{1,0:T(8,128)(2,1)S(1)} %bitcast.23, bf16[256,512]{1,0:T(8,128)(2,1)S(1)} %copy-done.6, f32[4,256,16]{2,1,0:T(8,128)S(1)} %bitcast.24, bf16[256,4096]{1,0:T(8,128)(2,1)S(1)} %copy-done.4), custom_call_target="tpu_custom_call" | custom-call | flops 2147483648 | bytes 11534336 | tf_op jit(solution)/shard_map/gated/pallas_call | solution.py:330
  133.9 9.4 %psum.7.sq_ref = f32[256,1]{1,0:T(8,128)S(1)} all-reduce(f32[256,1]{1,0:T(8,128)S(1)} %get-tuple-element.5), channel_id=1, replica_groups=mesh['ctx'=16,'tp'=2] {'tp'}, use_global_device_ids=true, to_apply=%region_3.4 | all-reduce | flops 256 | bytes 2048 | tf_op jit(solution)/shard_map/psum | solution.py:345
  143.3 2.2 copy-done.1
  145.5 2.3 %norm.1 = bf16[256,4096]{1,0:T(8,128)(2,1)} custom-call(f32[256,4096]{1,0:T(8,128)S(1)} %copy-done.1, f32[256,1]{1,0:T(8,128)S(1)} %psum.7.sq_ref, bf16[1,4096]{1,0:T(2,128)(2,1)S(1)} %broadcast_in_dim.50.gain_ref), custom_call_target="tpu_custom_call" | custom-call | tf_op jit(solution)/shard_map/norm/pallas_call | solution.py:346
  147.8 1.6 copy-done.11
  149.5 16.7 %attend.4.refs_2_ = bf16[256,4096]{1,0:T(8,128)(2,1)} custom-call(bf16[4096,256]{1,0:T(8,128)(2,1)S(1)} %copy-done.11, bf16[256,4096]{1,0:T(8,128)(2,1)S(1)} %copy-done.10), custom_call_target="tpu_custom_call" | custom-call | flops 8589934592 | bytes 2097152 | tf_op jit(solution)/shard_map/attend/pallas_call | solution.py:107
  166.2 1.6 copy-done.12
  167.8 16.5 %attend.5.refs_2_ = bf16[256,4096]{1,0:T(8,128)(2,1)} custom-call(bf16[4096,256]{1,0:T(8,128)(2,1)S(1)} %copy-done.12, bf16[256,4096]{1,0:T(8,128)(2,1)S(1)} %copy-done.10, bf16[256,4096]{1,0:T(8,128)(2,1)} %attend.4.refs_2_), custom_call_target="tpu_custom_call", output_to_operand_aliasing={{}: (2, {})} | custom-call | flops 8589934592 | bytes 2097152 | tf_op jit(solution)/shard_map/attend/pallas_call | solution.py:107
  184.3 1.6 copy-done.13
  185.9 16.5 %attend.6.refs_2_ = bf16[256,4096]{1,0:T(8,128)(2,1)} custom-call(bf16[4096,256]{1,0:T(8,128)(2,1)S(1)} %copy-done.13, bf16[256,4096]{1,0:T(8,128)(2,1)S(1)} %copy-done.10, bf16[256,4096]{1,0:T(8,128)(2,1)} %attend.5.refs_2_), custom_call_target="tpu_custom_call", output_to_operand_aliasing={{}: (2, {})} | custom-call | flops 8589934592 | bytes 2097152 | tf_op jit(solution)/shard_map/attend/pallas_call | solution.py:107
  202.5 1.6 copy-done.14
  204.0 16.5 %attend.7 = bf16[256,4096]{1,0:T(8,128)(2,1)} custom-call(bf16[4096,256]{1,0:T(8,128)(2,1)S(1)} %copy-done.14, bf16[256,4096]{1,0:T(8,128)(2,1)S(1)} %copy-done.10, bf16[256,4096]{1,0:T(8,128)(2,1)} %attend.6.refs_2_), custom_call_target="tpu_custom_call", output_to_operand_aliasing={{}: (2, {})} | custom-call | flops 8589934592 | bytes 2097152 | tf_op jit(solution)/shard_map/attend/pallas_call | solution.py:107
  (64 shorter events, 0.9 us)
Async XLA Ops:
  7.2 4.2 %copy-start = (f32[64,256]{1,0:T(8,128)S(1)}, f32[64,256]{1,0:T(8,128)}, u32[]{:S(2)}) copy-start(f32[64,256]{1,0:T(8,128)} %param.19) | copy-start | bytes 196612
  7.2 4.7 %copy-start.7 = (f32[64,256]{1,0:T(8,128)S(1)}, f32[64,256]{1,0:T(8,128)}, u32[]{:S(2)}) copy-start(f32[64,256]{1,0:T(8,128)} %param.18) | copy-start | bytes 196612
  7.2 5.6 %copy-start.5 = (bf16[256,512]{1,0:T(8,128)(2,1)S(1)}, bf16[256,512]{1,0:T(8,128)(2,1)}, u32[]{:S(2)}) copy-start(bf16[256,512]{1,0:T(8,128)(2,1)} %b_ref.3) | copy-start | bytes 786436
  7.2 140.6 %all-gather.12.cloned.1.call-start = ((), (), s32[]{:S(2)}) async-start(), calls=%async_computation.3 | async-start | bytes 2228224 | tf_op jit(solution)/shard_map/all_gather | solution.py:265
  9.8 156.4 %all-gather.10.cloned.1.call-start = ((), (), s32[]{:S(2)}) async-start(), calls=%async_computation.2 | async-start | bytes 2228224 | tf_op jit(solution)/shard_map/all_gather | solution.py:265
  10.5 173.8 %all-gather.8.cloned.1.call-start = ((), (), s32[]{:S(2)}) async-start(), calls=%async_computation.1 | async-start | bytes 2228224 | tf_op jit(solution)/shard_map/all_gather | solution.py:265
  11.3 191.2 %all-gather.6.cloned.1.call-start = ((), (), s32[]{:S(2)}) async-start(), calls=%async_computation | async-start | bytes 2228224 | tf_op jit(solution)/shard_map/all_gather | solution.py:265
  12.8 1.6 copy-start.2
  14.4 5.7 %copy-start.20 = (u32[32]{0:T(128)S(1)}, u32[32]{0:T(128)}, u32[]{:S(2)}) copy-start(u32[32]{0:T(128)} %constant.54) | copy-start | bytes 388
  20.0 27.0 %collective-permute-start = (bf16[32,64,128]{2,1,0:T(8,128)(2,1)S(1)}, bf16[32,64,128]{2,1,0:T(8,128)(2,1)S(1)}, u32[]{:S(2)}, u32[]{:S(2)}) collective-permute-start(bf16[32,64,128]{2,1,0:T(8,128)(2,1)S(1)} %bitcast.34), channel_id=1, source_target_pairs={{0,2},{2,0},{4,6},{6,4},{8,10},{10,8},{12,14},{14,12},{16,18},{18,... | collective-permute-start | bytes 1572872 | tf_op jit(solution)/shard_map/ppermute | solution.py:29
  46.9 39.4 %copy-start.15 = (f32[2048,128]{1,0:T(8,128)}, f32[2048,128]{1,0:T(8,128)S(1)}, u32[]{:S(2)}) copy-start(f32[2048,128]{1,0:T(8,128)S(1)} %slice_select_fusion) | copy-start | bytes 3145732
  46.9 39.3 %copy-start.16 = (bf16[32,64,128]{2,1,0:T(8,128)(2,1)}, bf16[32,64,128]{2,1,0:T(8,128)(2,1)S(1)}, u32[]{:S(2)}) copy-start(bf16[32,64,128]{2,1,0:T(8,128)(2,1)S(1)} %collective-permute-done) | copy-start | bytes 1572868
  47.2 18.2 %collective-permute-start.1 = (bf16[32,64,128]{2,1,0:T(8,128)(2,1)S(1)}, bf16[32,64,128]{2,1,0:T(8,128)(2,1)S(1)}, u32[]{:S(2)}, u32[]{:S(2)}) collective-permute-start(bf16[32,64,128]{2,1,0:T(8,128)(2,1)S(1)} %fusion.9), channel_id=1, source_target_pairs={{0,4},{2,6},{4,8},{6,10},{8,12},{10,14},{12,16},{14,18},{16,20},{1... | collective-permute-start | bytes 1572872 | tf_op jit(solution)/shard_map/ppermute | solution.py:25
  65.8 27.4 %copy-start.17 = (bf16[256,128]{1,0:T(8,128)(2,1)S(1)}, bf16[256,128]{1,0:T(8,128)(2,1)}, u32[]{:S(2)}) copy-start(bf16[256,128]{1,0:T(8,128)(2,1)} %get-tuple-element.13) | copy-start | bytes 196612
  65.8 27.4 %copy-start.18 = (bf16[256,128]{1,0:T(8,128)(2,1)S(1)}, bf16[256,128]{1,0:T(8,128)(2,1)}, u32[]{:S(2)}) copy-start(bf16[256,128]{1,0:T(8,128)(2,1)} %get-tuple-element.24) | copy-start | bytes 196612
  65.8 28.6 %copy-start.19 = (f32[64,256]{1,0:T(8,128)S(1)}, f32[64,256]{1,0:T(8,128)}, u32[]{:S(2)}) copy-start(f32[64,256]{1,0:T(8,128)} %get-tuple-element.19) | copy-start | bytes 196612
  65.8 20.4 %collective-permute-start.2 = (bf16[32,64,128]{2,1,0:T(8,128)(2,1)S(1)}, bf16[32,64,128]{2,1,0:T(8,128)(2,1)S(1)}, u32[]{:S(2)}, u32[]{:S(2)}) collective-permute-start(bf16[32,64,128]{2,1,0:T(8,128)(2,1)S(1)} %fusion.1), channel_id=1, source_target_pairs={{0,8},{2,10},{4,12},{6,14},{8,16},{10,18},{12,20},{14,22},{16,24},... | collective-permute-start | bytes 1572872 | tf_op jit(solution)/shard_map/ppermute | solution.py:25
  87.6 29.4 %collective-permute-start.3 = (bf16[32,64,128]{2,1,0:T(8,128)(2,1)}, bf16[32,64,128]{2,1,0:T(8,128)(2,1)}, u32[]{:S(2)}, u32[]{:S(2)}) collective-permute-start(bf16[32,64,128]{2,1,0:T(8,128)(2,1)} %add_convert_fusion), channel_id=1, source_target_pairs={{0,4},{2,6},{4,8},{6,10},{8,12},{10,14},{12,16},{14,18},{16,20},{1... | collective-permute-start | bytes 1572872 | tf_op jit(solution)/shard_map/ppermute | solution.py:25
  91.9 25.0 %collective-permute-start.4 = (bf16[32,64,128]{2,1,0:T(8,128)(2,1)}, bf16[32,64,128]{2,1,0:T(8,128)(2,1)}, u32[]{:S(2)}, u32[]{:S(2)}) collective-permute-start(bf16[32,64,128]{2,1,0:T(8,128)(2,1)} %add_convert_fusion), channel_id=1, source_target_pairs={{0,20},{2,22},{4,24},{6,26},{8,28},{10,30},{1,21},{3,23},{5,25},{7... | collective-permute-start | bytes 1572872 | tf_op jit(solution)/shard_map/ppermute | solution.py:25
  94.7 24.5 %copy-start.3 = (bf16[256,4096]{1,0:T(8,128)(2,1)S(1)}, bf16[256,4096]{1,0:T(8,128)(2,1)}, u32[]{:S(2)}) copy-start(bf16[256,4096]{1,0:T(8,128)(2,1)} %x_ref.3) | copy-start | bytes 6291460
  97.8 21.4 %copy-start.6 = (bf16[256,512]{1,0:T(8,128)(2,1)S(1)}, bf16[256,512]{1,0:T(8,128)(2,1)}, u32[]{:S(2)}) copy-start(bf16[256,512]{1,0:T(8,128)(2,1)} %c_ref.3) | copy-start | bytes 786436
  97.8 21.4 %copy-start.8 = (f32[64,256]{1,0:T(8,128)S(1)}, f32[64,256]{1,0:T(8,128)}, u32[]{:S(2)}) copy-start(f32[64,256]{1,0:T(8,128)} %param.18) | copy-start | bytes 196612
  97.8 21.4 %copy-start.9 = (f32[1,4096]{1,0:T(1,128)S(1)}, f32[1,4096]{1,0:T(1,128)}, u32[]{:S(2)}) copy-start(f32[1,4096]{1,0:T(1,128)} %broadcast_in_dim_reshape.3.skip_ref) | copy-start | bytes 49156
  119.1 6.9 %collective-permute-start.5 = (bf16[32,64,128]{2,1,0:T(8,128)(2,1)S(1)}, bf16[32,64,128]{2,1,0:T(8,128)(2,1)S(1)}, u32[]{:S(2)}, u32[]{:S(2)}) collective-permute-start(bf16[32,64,128]{2,1,0:T(8,128)(2,1)S(1)} %get-tuple-element.10), channel_id=1, source_target_pairs={{0,2},{2,0},{4,6},{6,4},{8,10},{10,8},{12,14},{14,12},{16,18},{18,... | collective-permute-start | bytes 1572872 | tf_op jit(solution)/shard_map/ppermute | solution.py:29
  126.0 1.6 copy-start.4
  143.3 2.2 copy-start.1
  145.5 2.3 %copy-start.10 = (bf16[256,4096]{1,0:T(8,128)(2,1)S(1)}, bf16[256,4096]{1,0:T(8,128)(2,1)}, u32[]{:S(2)}) copy-start(bf16[256,4096]{1,0:T(8,128)(2,1)} %refs_1_.7) | copy-start | bytes 6291460
  147.8 1.6 copy-start.11
  166.2 1.6 copy-start.12
  184.3 1.6 copy-start.13
  202.5 1.6 copy-start.14
Sparse Core Ops, SparseCore 0:
  10.2 41.3 all-gather.11
  53.8 44.2 all-gather.9
  100.2 53.4 all-gather.7
  155.7 40.1 all-gather.5

commit v2 on v1

--- a/solution.py
+++ b/solution.py
@@ -12,7 +12,6 @@
 STATE_HEADS = 128
 P_SIZE = 64
 N = 128
-CHUNK = 1024
 HEADS_STEP = 4
 VMEM_LIMIT = 48 * 1024 * 1024
 
@@ -29,36 +28,104 @@
     return lax.ppermute(block, axis, [(i, i ^ 1) for i in range(lax.axis_size(axis))])
 
 
-def attend_kernel(chunk, *refs):
-    kv_ref, q_ref = refs[:2]
-    o_ref, m_scr, acc_scr = refs[-3:]
-    rows = q_ref.shape[0]
-    heads = q_ref.shape[1] // HEAD_WIDTH
+ROW = 4
+
+
+def attend_kernel(kv_ref, q_ref, o_ref, buf, m_scr, acc_scr, zs, zr, xs, xr, ps, pr, fs, fr):
+    groups, rows = kv_ref.shape[:2]
+    chunk = ROW * rows
+    per = q_ref.shape[1] // HEAD_WIDTH // groups
     factor = HEAD_WIDTH ** (-0.5) * math.log2(math.e)
-    q_start = lax.axis_index("ctx") * rows
-    last = q_start // chunk
-
-    def sweep(c, first):
-        start = pl.multiple_of(c * chunk, chunk)
-        keys = kv_ref[pl.ds(start, chunk), :HEAD_WIDTH]
-        values = kv_ref[pl.ds(start, chunk), HEAD_WIDTH:]
+    me = lax.axis_index("ctx")
+    lines = buf.shape[0]
+    line = me // ROW
+    place = me % ROW
+    core = me % 2
+    side = (me // 2) % 2
+    mate = me + 1 - 2 * core
+    across = me + 2 - 4 * side
+    across_place = place + 2 - 4 * side
+    steps = (line + 1) * groups
+
+    def slot(age, g, at):
+        return buf.at[age, g, pl.ds(pl.multiple_of(at * rows, rows), rows)]
+
+    def send(src, dst, a, b, to):
+        return pltpu.make_async_remote_copy(
+            src_ref=src,
+            dst_ref=dst,
+            send_sem=a,
+            recv_sem=b,
+            device_id={"ctx": to},
+            device_id_type=pl.DeviceIdType.MESH,
+        )
+
+    def down(age, g, to):
+        return send(kv_ref.at[g], slot(age, g, place), zs.at[age, g], zr.at[age, g], to)
+
+    def to_mate(age, g, src):
+        return send(src, slot(age, g, place), ps.at[age, g], pr.at[age, g], mate)
+
+    def to_across(age, g, src):
+        return send(src, slot(age, g, place), xs.at[age, g], xr.at[age, g], across)
+
+    def forward(age, g):
+        here = slot(age, g, across_place)
+        return send(here, here, fs.at[age, g], fr.at[age, g], mate)
+
+    barrier = pltpu.get_barrier_semaphore()
+    for d in range(1, lines):
+        other = ((line + d) % lines) * ROW + place
+        pl.semaphore_signal(
+            barrier, inc=1, device_id={"ctx": other}, device_id_type=pl.DeviceIdType.MESH
+        )
+    for other in (mate, across):
+        pl.semaphore_signal(
+            barrier, inc=1, device_id={"ctx": other}, device_id_type=pl.DeviceIdType.MESH
+        )
+    pl.semaphore_wait(barrier, lines + 1)
+
+    for g in range(groups):
+        to_across(0, g, kv_ref.at[g]).start()
+        to_mate(0, g, kv_ref.at[g]).start()
+    for d in range(1, lines):
+
+        @pl.when(line + d < lines)
+        def _():
+            for g in range(groups):
+                down(d, g, me + d * ROW).start()
+
+    for g in range(groups):
+        buf[0, g, pl.ds(pl.multiple_of(place * rows, rows), rows), :] = kv_ref[g]
+
+    def spread(t):
+        age, g = t // groups, t % groups
+        down(age, g, mate).wait_recv()
+        to_across(age, g, slot(age, g, place)).start()
+        to_mate(age, g, slot(age, g, place)).start()
+
+    def relay(t):
+        age, g = t // groups, t % groups
+        to_across(age, g, slot(age, g, place)).wait_recv()
+        forward(age, g).start()
+
+    def work(age, g, first):
+        keys = buf[age, g, :, :HEAD_WIDTH]
+        values = buf[age, g, :, HEAD_WIDTH:]
         values = jnp.concatenate([values, jnp.ones_like(values)], axis=1)
-        if first:
-            gap = lax.broadcasted_iota(jnp.int32, (rows, chunk), 0) - lax.broadcasted_iota(
-                jnp.int32, (rows, chunk), 1
-            )
-            valid = gap >= start - q_start
-
-        @pl.loop(0, heads // HEADS_STEP)
+
+        @pl.loop(0, per // HEADS_STEP)
         def _(outer):
             for inner in range(HEADS_STEP):
-                h = outer * HEADS_STEP + inner
+                h = g * per + outer * HEADS_STEP + inner
                 q = q_ref[:, pl.ds(pl.multiple_of(h * HEAD_WIDTH, HEAD_WIDTH), HEAD_WIDTH)]
                 s = lax.dot_general(
                     q, keys, (((1,), (1,)), ((), ())), preferred_element_type=jnp.float32
                 )
                 if first:
-                    s = jnp.where(valid, s, causal_score)
+                    gap = lax.broadcasted_iota(jnp.int32, (rows, chunk), 0)
+                    gap = gap - lax.broadcasted_iota(jnp.int32, (rows, chunk), 1)
+                    s = jnp.where(gap >= -place * rows, s, causal_score)
                 top = jnp.max(s, axis=1, keepdims=True)
                 if first:
                     p = jnp.exp2((s - top) * factor)
@@ -76,51 +143,68 @@
                     acc_scr[h, :, HEAD_WIDTH:] = acc_scr[h, :, HEAD_WIDTH:] * a + r[:, HEAD_WIDTH:]
                     m_scr[h] = new
 
-    sweep(last, True)
-
-    @pl.loop(0, last)
-    def _(c):
-        sweep(c, False)
-
-    for h in range(heads):
-        o_ref[:, h * HEAD_WIDTH : (h + 1) * HEAD_WIDTH] = (
+    for t in range(groups, 2):
+        pl.when(t < steps)(functools.partial(spread, t))
+    relay(0)
+
+    @pl.loop(0, steps)
+    def _(s):
+        pl.when((s + 2 < steps) & (s + 2 >= groups))(lambda: spread(s + 2))
+        pl.when(s + 1 < steps)(lambda: relay(s + 1))
+        age, g = s // groups, s % groups
+        to_mate(age, g, slot(age, g, place)).wait_recv()
+        forward(age, g).wait_recv()
+        pl.when(age == 0)(lambda: work(0, g, True))
+        pl.when(age > 0)(lambda: work(age, g, False))
+
+    @pl.loop(0, steps)
+    def _(s):
+        age, g = s // groups, s % groups
+        to_across(age, g, slot(age, g, place)).wait_send()
+        to_mate(age, g, slot(age, g, place)).wait_send()
+        forward(age, g).wait_send()
+
+    for d in range(1, lines):
+
+        @pl.when(line + d < lines)
+        def _():
+            for g in range(groups):
+                down(d, g, mate).wait_send()
+
+    @pl.loop(0, per * groups)
+    def _(h):
+        o_ref[:, pl.ds(pl.multiple_of(h * HEAD_WIDTH, HEAD_WIDTH), HEAD_WIDTH)] = (
             acc_scr[h, :, :HEAD_WIDTH] / acc_scr[h, :, HEAD_WIDTH:]
         ).astype(o_ref.dtype)
 
 
-def attend(kv, queries, so_far, head, kv_heads):
-    rows, width = queries.shape
-    cols = width // kv_heads
-    keys = kv.shape[0]
-    chunk = CHUNK if keys % CHUNK == 0 and CHUNK % rows == 0 else rows
-    q_heads = cols // HEAD_WIDTH
-    in_specs = [
-        pl.BlockSpec((keys, 2 * HEAD_WIDTH), lambda i: (0, 0)),
-        pl.BlockSpec((rows, cols), lambda i: (0, head)),
-    ]
-    operands = [kv, queries]
-    aliases = {}
-    if so_far is not None:
-        in_specs.append(pl.BlockSpec(memory_space=pl.ANY))
-        operands.append(so_far)
-        aliases = {2: 0}
+def attend(kv, queries):
+    groups, rows, both = kv.shape
+    lines = lax.axis_size("ctx") // ROW
+    heads = queries.shape[1] // HEAD_WIDTH
+    vmem = pl.BlockSpec(memory_space=pltpu.VMEM)
+    sems = pltpu.SemaphoreType.DMA((lines, groups))
     return pl.pallas_call(
-        functools.partial(attend_kernel, chunk),
-        grid=(1,),
-        out_shape=jax.ShapeDtypeStruct((rows, width), jnp.bfloat16),
-        in_specs=in_specs,
-        out_specs=pl.BlockSpec((rows, cols), lambda i: (0, head)),
+        attend_kernel,
+        out_shape=jax.ShapeDtypeStruct(queries.shape, jnp.bfloat16),
+        in_specs=[vmem, vmem],
+        out_specs=vmem,
         scratch_shapes=[
-            pltpu.VMEM((q_heads, rows, HEAD_WIDTH), jnp.float32),
-            pltpu.VMEM((q_heads, rows, 2 * HEAD_WIDTH), jnp.float32),
-        ],
-        input_output_aliases=aliases,
-        compiler_params=pltpu.CompilerParams(vmem_limit_bytes=VMEM_LIMIT),
+            pltpu.VMEM((lines, groups, ROW * rows, both), jnp.bfloat16),
+            pltpu.VMEM((heads, rows, HEAD_WIDTH), jnp.float32),
+            pltpu.VMEM((heads, rows, 2 * HEAD_WIDTH), jnp.float32),
+        ]
+        + [sems] * 8,
+        compiler_params=pltpu.CompilerParams(
+            vmem_limit_bytes=VMEM_LIMIT, collective_id=0, has_side_effects=True
+        ),
         cost_estimate=pl.CostEstimate(
-            flops=8 * rows * keys * cols, bytes_accessed=4 * keys * HEAD_WIDTH, transcendentals=0
+            flops=40 * rows * rows * heads * HEAD_WIDTH * lines,
+            bytes_accessed=8 << 20,
+            transcendentals=0,
         ),
         name="attend",
-    )(*operands)
+    )(kv, queries)
 
 
 def pair_select(rows, first, second):
@@ -258,11 +342,9 @@
 ):
     rows = queries.shape[0]
     kv_heads = key_rows.shape[1] // HEAD_WIDTH
-    gathered = []
-    for g in range(kv_heads):
-        cols = slice(g * HEAD_WIDTH, (g + 1) * HEAD_WIDTH)
-        both = jnp.concatenate([key_rows[:, cols], value_head_rows[:, cols]], axis=1)
-        gathered.append(lax.all_gather(both, "ctx", axis=0, tiled=True))
+    kv = jnp.stack([key_rows, value_head_rows], axis=1)
+    kv = kv.reshape(rows, 2, kv_heads, HEAD_WIDTH).transpose(2, 0, 1, 3)
+    kv = kv.reshape(kv_heads, rows, 2 * HEAD_WIDTH)
 
     heads = step_size.shape[0]
     groups = b_matrix.shape[1] // N
@@ -323,9 +405,7 @@
         jnp.repeat(skip_gain, P_SIZE)[None, :],
     )
 
-    attention_out = None
-    for g in range(kv_heads):
-        attention_out = attend(gathered[g], queries, attention_out, g, kv_heads)
+    attention_out = attend(kv, queries)
 
     gated, square = pl.pallas_call(
         gate_kernel,

time: 231 us -> 225 us (0.974); the launches traced: 227 us -> 224 us
  Pallas kernels: 87.3 us -> 126 us
  waiting for transfers between devices: 49.5 us -> 22.4 us
  between operations: 14.8 us -> 1.74 us
    pallas_call x4 -> x1, Pallas kernels: 66.3 us -> 105 us  [attend(): pl.pallas_call(attend_kernel, out_shape=jax.ShapeDtypeStruct(queries.shap...]
    ppermute x4, waiting for transfers between devices: 49.4 us -> 22.4 us  [passed_along(): return lax.ppermute(block, axis, route)]
    concatenate x4 -> x0, other arithmetic: 2.68 us -> none  [local(): jnp.concatenate([key_rows[:, cols], value_head_rows[:, cols]], axis=1)]
    unnamed x45 -> x42, local copies, waits for them, and re-layouts: 12.5 us -> 10.5 us
  transfers between devices with their start and end apart: 10 -> 6, of which waited for: 3 -> 2; matrix products, arithmetic and copies ran while one was open for 6% -> 5% of each run, Pallas kernels for 31% -> 50%
where the time goes in v2:
time: 225 us; the launch traced here: 224 us
  Pallas kernels  126 us (56%)
  blocking collectives  34.2 us (15%)
  waiting for transfers between devices  22.4 us (10%)
  local copies, waits for them, and re-layouts  18.6 us (8%)
  starting transfers between devices  11.4 us (5%)
  other arithmetic  9.77 us (4%)
    pallas_call x1, Pallas kernels, attend(): pl.pallas_call(attend_kernel, out_shape=jax.ShapeDtypeStruct(queries.shap...  105 us
    unnamed x1, blocking collectives  24.4 us
    ppermute x4, waiting for transfers between devices, passed_along(): return lax.ppermute(block, axis, route)  22.4 us
    ppermute x4, starting transfers between devices, passed_along(): return lax.ppermute(block, axis, route)  11.2 us
    unnamed x42, local copies, waits for them, and re-layouts  10.5 us
    psum x1, blocking collectives, local(): square = lax.psum(square, 'tp')  9.83 us
    pallas_call x1, Pallas kernels, local(): pl.pallas_call(inner_kernel, grid=(groups,), in_specs=[wide, narrow, narr...  6.82 us
    pallas_call x1, Pallas kernels, local(): pl.pallas_call(gate_kernel, grid=(groups,), in_specs=[wide, state, narrow...  6.38 us
  transfers between devices with their start and end apart: 6, of which 2 were waited for; matrix products, arithmetic and copies ran while one was open for 5% of the time, Pallas kernels for 50%

profile of v2, /device:TPU:24, one launch (start us, length us, event | category | flops | bytes accessed | tf_op | source)
XLA Modules:
  0.0 224.0 jit_solution(2927899561875716376)
XLA Ops:
  0.7 0.8 copy-done
  1.5 0.4 fusion.2
  1.8 0.2 slice_reduce_fusion
  2.0 0.9 bitcast_exponential_fusion
  3.0 0.2 copy.19
  3.2 1.6 copy-done.2
  4.8 0.9 copy-done.7
  5.7 5.5 %local_state.1 = f32[4096,128]{1,0:T(8,128)S(1)} custom-call(bf16[256,4096]{1,0:T(8,128)(2,1)S(1)} %copy-done.2, bf16[256,512]{1,0:T(8,128)(2,1)S(1)} %copy-done.7, f32[4,256,16]{2,1,0:T(8,128)S(1)} %bitcast.27), custom_call_target="tpu_custom_call" | custom-call | flops 1073741824 | bytes 4194304 | tf_op jit(solution)/shard_map/local_state/pallas_call | solution.py:372
  11.2 0.1 select_convert_fusion.2
  11.4 0.6 dynamic-slice
  12.7 0.2 dynamic-update-slice
  12.9 24.4 %all-reduce = f32[1024]{0:T(1024)S(1)} all-reduce(f32[1024]{0:T(1024)S(1)} %dynamic-update-slice), channel_id=2, replica_groups=mesh['ctx'=16,'tp'=2] {'ctx'}, use_global_device_ids=true, to_apply=%add | all-reduce | flops 1024 | bytes 8192
  37.3 0.1 reshape.102
  37.4 0.1 slice_select_fusion.1
  37.5 0.5 exponential_bitcast_fusion
  38.0 0.1 slice_select_fusion
  38.1 0.3 fusion.9
  38.4 5.8 %collective-permute-start.1 = (bf16[32,64,128]{2,1,0:T(8,128)(2,1)S(1)}, bf16[32,64,128]{2,1,0:T(8,128)(2,1)S(1)}, u32[]{:S(2)}, u32[]{:S(2)}) collective-permute-start(bf16[32,64,128]{2,1,0:T(8,128)(2,1)S(1)} %fusion.9), channel_id=1, source_target_pairs={{0,4},{2,6},{4,8},{6,10},{8,12},{10,14},{12,16},{14,18},{16,20},{1... | collective-permute-start | bytes 1572872 | tf_op jit(solution)/shard_map/ppermute | solution.py:24
  44.3 0.1 select_reduce_fusion
  44.4 11.2 %collective-permute-done.1 = bf16[32,64,128]{2,1,0:T(8,128)(2,1)S(1)} collective-permute-done((bf16[32,64,128]{2,1,0:T(8,128)(2,1)S(1)}, bf16[32,64,128]{2,1,0:T(8,128)(2,1)S(1)}, u32[]{:S(2)}, u32[]{:S(2)}) %collective-permute-start.1) | collective-permute-done | bytes 524320 | tf_op jit(solution)/shard_map/ppermute | solution.py:24
  55.6 1.2 fusion.1
  56.7 1.3 collective-permute-start.2
  58.1 0.4 copy.16
  58.6 0.4 copy.17
  59.0 1.9 maximum_bitcast_fusion
  60.9 1.5 reshape.96.kv_ref
  62.4 11.2 %collective-permute-done.2 = bf16[32,64,128]{2,1,0:T(8,128)(2,1)} collective-permute-done((bf16[32,64,128]{2,1,0:T(8,128)(2,1)}, bf16[32,64,128]{2,1,0:T(8,128)(2,1)}, u32[]{:S(2)}, u32[]{:S(2)}) %collective-permute-start.2) | collective-permute-done | bytes 524320 | tf_op jit(solution)/shard_map/ppermute | solution.py:24
  73.6 2.8 %add_convert_fusion = bf16[32,64,128]{2,1,0:T(8,128)(2,1)} fusion(bf16[32,64,128]{2,1,0:T(8,128)(2,1)} %collective-permute-done.2, bf16[32,64,128]{2,1,0:T(8,128)(2,1)} %copy-done.15, f32[32]{0:T(128)S(1)} %exp.51, f32[32]{0:T(128)S(1)} %exp.50, f32[32,64,128]{2,1,0:T(8,128)} %bitcast.34, bf16[32,64,128]{2,1,0:T(8,128)(2,1)S(1)} %collective-permute-done, ...), kind=kLoop, calls=%fused_computation.8 | loop fusion | flops 3145728 | bytes 3146113 | tf_op jit(solution)/shard_map/convert_element_type | solution.py:317
  76.4 2.8 %collective-permute-start.3 = (bf16[32,64,128]{2,1,0:T(8,128)(2,1)}, bf16[32,64,128]{2,1,0:T(8,128)(2,1)}, u32[]{:S(2)}, u32[]{:S(2)}) collective-permute-start(bf16[32,64,128]{2,1,0:T(8,128)(2,1)} %add_convert_fusion), channel_id=1, source_target_pairs={{0,4},{2,6},{4,8},{6,10},{8,12},{10,14},{12,16},{14,18},{16,20},{1... | collective-permute-start | bytes 1572872 | tf_op jit(solution)/shard_map/ppermute | solution.py:24
  79.3 1.3 collective-permute-start.4
  80.6 104.6 %attend.1 = bf16[256,4096]{1,0:T(8,128)(2,1)S(1)} custom-call(bf16[4,256,256]{2,1,0:T(8,128)(2,1)S(1)} %reshape.96.kv_ref, bf16[256,4096]{1,0:T(8,128)(2,1)S(1)} %copy-done.12), custom_call_target="tpu_custom_call" | custom-call | flops 42949672960 | bytes 8388608 | tf_op jit(solution)/shard_map/attend/pallas_call | solution.py:187
  185.3 1.3 copy-done.4
  186.6 0.6 exp.52
  187.2 0.2 copy.20
  187.4 0.2 copy.18.ccol_ref
  187.6 1.5 broadcast_in_dim.45
  189.1 1.4 broadcast_in_dim_reshape.3.skip_ref
  190.5 0.8 broadcast_in_dim.50.gain_ref
  191.3 2.2 select_convert_fusion.1
  193.4 0.1 collective-permute-start.5
  193.6 6.8 %inner.1.y_ref = f32[256,4096]{1,0:T(8,128)} custom-call(bf16[256,4096]{1,0:T(8,128)(2,1)S(1)} %copy-done.3, bf16[256,512]{1,0:T(8,128)(2,1)S(1)} %copy-done.8, bf16[256,512]{1,0:T(8,128)(2,1)S(1)} %copy-done.9, f32[4,256,16]{2,1,0:T(8,128)S(1)} %copy.18.ccol_ref, f32[4,16,256]{2,1,0:T(8,128)S(1)} %bitcast.30, f32[4,16,256]{2,1,0:T(8,128)S(1)} %bitcast.31, ...), custom_call_target="tpu_custom_call" | custom-call | flops 10737418240 | bytes 6291456 | tf_op jit(solution)/shard_map/inner/pallas_call | solution.py:387
  200.4 0.2 maximum_select_fusion
  200.6 1.4 copy-done.6
  202.0 6.4 %gated.1 = (f32[256,4096]{1,0:T(8,128)}, f32[256,1]{1,0:T(8,128)S(1)}) custom-call(f32[256,4096]{1,0:T(8,128)} %inner.1.y_ref, bf16[4096,128]{1,0:T(8,128)(2,1)S(1)} %bitcast.25, bf16[256,512]{1,0:T(8,128)(2,1)S(1)} %copy-done.9, f32[4,256,16]{2,1,0:T(8,128)S(1)} %bitcast.26, bf16[256,4096]{1,0:T(8,128)(2,1)S(1)} %copy-done.6), custom_call_target="tpu_custom_call" | custom-call | flops 2147483648 | bytes 11534336 | tf_op jit(solution)/shard_map/gated/pallas_call | solution.py:410
  208.4 9.8 %psum.7.sq_ref = f32[256,1]{1,0:T(8,128)S(1)} all-reduce(f32[256,1]{1,0:T(8,128)S(1)} %get-tuple-element.5), channel_id=1, replica_groups=mesh['ctx'=16,'tp'=2] {'tp'}, use_global_device_ids=true, to_apply=%region_3.4 | all-reduce | flops 256 | bytes 2048 | tf_op jit(solution)/shard_map/psum | solution.py:425
  218.2 2.2 copy-done.1
  220.4 2.3 %norm.1 = bf16[256,4096]{1,0:T(8,128)(2,1)} custom-call(f32[256,4096]{1,0:T(8,128)S(1)} %copy-done.1, f32[256,1]{1,0:T(8,128)S(1)} %psum.7.sq_ref, bf16[1,4096]{1,0:T(2,128)(2,1)S(1)} %broadcast_in_dim.50.gain_ref), custom_call_target="tpu_custom_call" | custom-call | tf_op jit(solution)/shard_map/norm/pallas_call | solution.py:426
  222.7 1.3 copy.23
  (47 shorter events, 0.3 us)
Async XLA Ops:
  0.6 0.8 copy-start
  3.2 1.6 copy-start.2
  4.8 0.9 copy-start.7
  5.7 5.7 %copy-start.18 = (u32[32]{0:T(128)S(1)}, u32[32]{0:T(128)}, u32[]{:S(2)}) copy-start(u32[32]{0:T(128)} %constant.54) | copy-start | bytes 388
  11.3 26.8 %collective-permute-start = (bf16[32,64,128]{2,1,0:T(8,128)(2,1)S(1)}, bf16[32,64,128]{2,1,0:T(8,128)(2,1)S(1)}, u32[]{:S(2)}, u32[]{:S(2)}) collective-permute-start(bf16[32,64,128]{2,1,0:T(8,128)(2,1)S(1)} %bitcast.36), channel_id=1, source_target_pairs={{0,2},{2,0},{4,6},{6,4},{8,10},{10,8},{12,14},{14,12},{16,18},{18,... | collective-permute-start | bytes 1572872 | tf_op jit(solution)/shard_map/ppermute | solution.py:28
  38.1 18.6 %copy-start.13 = (f32[2048,128]{1,0:T(8,128)}, f32[2048,128]{1,0:T(8,128)S(1)}, u32[]{:S(2)}) copy-start(f32[2048,128]{1,0:T(8,128)S(1)} %slice_select_fusion) | copy-start | bytes 3145732
  38.1 35.5 %copy-start.14 = (bf16[32,64,128]{2,1,0:T(8,128)(2,1)}, bf16[32,64,128]{2,1,0:T(8,128)(2,1)S(1)}, u32[]{:S(2)}) copy-start(bf16[32,64,128]{2,1,0:T(8,128)(2,1)S(1)} %collective-permute-done) | copy-start | bytes 1572868
  38.1 19.9 %copy-start.16 = (bf16[256,512]{1,0:T(8,128)(2,1)S(1)}, bf16[256,512]{1,0:T(8,128)(2,1)}, u32[]{:S(2)}) copy-start(bf16[256,512]{1,0:T(8,128)(2,1)} %param.12) | copy-start | bytes 786436
  38.4 20.1 %copy-start.17 = (bf16[256,512]{1,0:T(8,128)(2,1)S(1)}, bf16[256,512]{1,0:T(8,128)(2,1)}, u32[]{:S(2)}) copy-start(bf16[256,512]{1,0:T(8,128)(2,1)} %param.13) | copy-start | bytes 786436
  38.4 17.1 %collective-permute-start.1 = (bf16[32,64,128]{2,1,0:T(8,128)(2,1)S(1)}, bf16[32,64,128]{2,1,0:T(8,128)(2,1)S(1)}, u32[]{:S(2)}, u32[]{:S(2)}) collective-permute-start(bf16[32,64,128]{2,1,0:T(8,128)(2,1)S(1)} %fusion.9), channel_id=1, source_target_pairs={{0,4},{2,6},{4,8},{6,10},{8,12},{10,14},{12,16},{14,18},{16,20},{1... | collective-permute-start | bytes 1572872 | tf_op jit(solution)/shard_map/ppermute | solution.py:24
  55.6 2.5 %copy-start.15 = (bf16[32,64,128]{2,1,0:T(8,128)(2,1)}, bf16[32,64,128]{2,1,0:T(8,128)(2,1)S(1)}, u32[]{:S(2)}) copy-start(bf16[32,64,128]{2,1,0:T(8,128)(2,1)S(1)} %collective-permute-done.1) | copy-start | bytes 1572868
  56.7 16.9 %collective-permute-start.2 = (bf16[32,64,128]{2,1,0:T(8,128)(2,1)}, bf16[32,64,128]{2,1,0:T(8,128)(2,1)}, u32[]{:S(2)}, u32[]{:S(2)}) collective-permute-start(bf16[32,64,128]{2,1,0:T(8,128)(2,1)} %fusion.1), channel_id=1, source_target_pairs={{0,8},{2,10},{4,12},{6,14},{8,16},{10,18},{12,20},{14,22},{16,24},... | collective-permute-start | bytes 1572872 | tf_op jit(solution)/shard_map/ppermute | solution.py:24
  60.9 19.7 %copy-start.12 = (bf16[256,4096]{1,0:T(8,128)(2,1)S(1)}, bf16[256,4096]{1,0:T(8,128)(2,1)}, u32[]{:S(2)}) copy-start(bf16[256,4096]{1,0:T(8,128)(2,1)} %q_ref.1) | copy-start | bytes 6291460
  76.4 114.8 %collective-permute-start.3 = (bf16[32,64,128]{2,1,0:T(8,128)(2,1)}, bf16[32,64,128]{2,1,0:T(8,128)(2,1)}, u32[]{:S(2)}, u32[]{:S(2)}) collective-permute-start(bf16[32,64,128]{2,1,0:T(8,128)(2,1)} %add_convert_fusion), channel_id=1, source_target_pairs={{0,4},{2,6},{4,8},{6,10},{8,12},{10,14},{12,16},{14,18},{16,20},{1... | collective-permute-start | bytes 1572872 | tf_op jit(solution)/shard_map/ppermute | solution.py:24
  79.3 112.0 %collective-permute-start.4 = (bf16[32,64,128]{2,1,0:T(8,128)(2,1)}, bf16[32,64,128]{2,1,0:T(8,128)(2,1)}, u32[]{:S(2)}, u32[]{:S(2)}) collective-permute-start(bf16[32,64,128]{2,1,0:T(8,128)(2,1)} %add_convert_fusion), channel_id=1, source_target_pairs={{0,20},{2,22},{4,24},{6,26},{8,28},{10,30},{1,21},{3,23},{5,25},{7... | collective-permute-start | bytes 1572872 | tf_op jit(solution)/shard_map/ppermute | solution.py:24
  185.3 1.3 copy-start.4
  187.4 6.2 %copy-start.3 = (bf16[256,4096]{1,0:T(8,128)(2,1)S(1)}, bf16[256,4096]{1,0:T(8,128)(2,1)}, u32[]{:S(2)}) copy-start(bf16[256,4096]{1,0:T(8,128)(2,1)} %x_ref.3) | copy-start | bytes 6291460
  187.4 6.2 %copy-start.8 = (bf16[256,512]{1,0:T(8,128)(2,1)S(1)}, bf16[256,512]{1,0:T(8,128)(2,1)}, u32[]{:S(2)}) copy-start(bf16[256,512]{1,0:T(8,128)(2,1)} %b_ref.3) | copy-start | bytes 786436
  190.5 3.0 %copy-start.9 = (bf16[256,512]{1,0:T(8,128)(2,1)S(1)}, bf16[256,512]{1,0:T(8,128)(2,1)}, u32[]{:S(2)}) copy-start(bf16[256,512]{1,0:T(8,128)(2,1)} %c_ref.3) | copy-start | bytes 786436
  190.5 3.1 %copy-start.10 = (f32[64,256]{1,0:T(8,128)S(1)}, f32[64,256]{1,0:T(8,128)}, u32[]{:S(2)}) copy-start(f32[64,256]{1,0:T(8,128)} %param.18) | copy-start | bytes 196612
  190.5 3.1 %copy-start.11 = (f32[1,4096]{1,0:T(1,128)S(1)}, f32[1,4096]{1,0:T(1,128)}, u32[]{:S(2)}) copy-start(f32[1,4096]{1,0:T(1,128)} %broadcast_in_dim_reshape.3.skip_ref) | copy-start | bytes 49156
  193.4 7.0 %collective-permute-start.5 = (bf16[32,64,128]{2,1,0:T(8,128)(2,1)S(1)}, bf16[32,64,128]{2,1,0:T(8,128)(2,1)S(1)}, u32[]{:S(2)}, u32[]{:S(2)}) collective-permute-start(bf16[32,64,128]{2,1,0:T(8,128)(2,1)S(1)} %get-tuple-element.10), channel_id=1, source_target_pairs={{0,2},{2,0},{4,6},{6,4},{8,10},{10,8},{12,14},{14,12},{16,18},{18,... | collective-permute-start | bytes 1572872 | tf_op jit(solution)/shard_map/ppermute | solution.py:28
  200.4 1.6 copy-start.6
  218.2 2.2 copy-start.1
  220.4 2.3 %copy-start.5 = (bf16[256,4096]{1,0:T(8,128)(2,1)S(1)}, bf16[256,4096]{1,0:T(8,128)(2,1)}, u32[]{:S(2)}) copy-start(bf16[256,4096]{1,0:T(8,128)(2,1)} %copy-done.4) | copy-start | bytes 6291460

commit v3 on v2

--- a/solution.py
+++ b/solution.py
@@ -18,20 +18,13 @@
 causal_score = -1e30
 
 
-def passed_along(block, axis, distance):
-    devices = range(lax.axis_size(axis))
-    route = [(i - distance, i) for i in devices if i - distance in devices]
-    return lax.ppermute(block, axis, route)
-
-
-def swapped(block, axis):
-    return lax.ppermute(block, axis, [(i, i ^ 1) for i in range(lax.axis_size(axis))])
-
-
 ROW = 4
 
 
-def attend_kernel(kv_ref, q_ref, o_ref, buf, m_scr, acc_scr, zs, zr, xs, xr, ps, pr, fs, fr):
+def attend_kernel(
+    widths, kv_ref, q_ref, st_ref, dec_ref, o_ref, in_ref, buf, m_scr, acc_scr, zs, zr, xs, xr,
+    ps, pr, fs, fr, out_buf, in_buf, dec_out, dec_in, total, lead, dec_tot, dec_lead, ss, sr, ds, dr
+):
     groups, rows = kv_ref.shape[:2]
     chunk = ROW * rows
     per = q_ref.shape[1] // HEAD_WIDTH // groups
@@ -83,7 +76,160 @@
         pl.semaphore_signal(
             barrier, inc=1, device_id={"ctx": other}, device_id_type=pl.DeviceIdType.MESH
         )
-    pl.semaphore_wait(barrier, lines + 1)
+    count = lines * ROW
+    far = 1 + 2 * widths[-1] if widths else 2
+    far_offset = 2 * far
+    for other in (
+        (me + 2) % count,
+        (me + count - 2) % count,
+        (me + far_offset) % count,
+        (me + count - far_offset) % count,
+    ):
+        pl.semaphore_signal(
+            barrier, inc=1, device_id={"ctx": other}, device_id_type=pl.DeviceIdType.MESH
+        )
+    pl.semaphore_wait(barrier, lines + 5)
+
+    half = st_ref.shape[0] // 2
+    pair = me // 2
+    pairs = count // 2
+    mine, other_half = core * half, (1 - core) * half
+    near_slot = 1 + len(widths)
+    far_slot, last_slot = near_slot + 1, near_slot + 2
+
+    def state_copy(k, src_k, to):
+        return send(out_buf.at[src_k], in_buf.at[k], ss.at[k], sr.at[k], to)
+
+    def decay_copy(k, src_k, to):
+        return send(dec_out.at[src_k], dec_in.at[k], ds.at[k], dr.at[k], to)
+
+    def pass_on(k, distance):
+        @pl.when(pair + distance < pairs)
+        def _():
+            state_copy(k, k, me + 2 * distance).start()
+            decay_copy(k, k, me + 2 * distance).start()
+
+    def pass_to_all(k):
+        if k < near_slot:
+            pass_on(k, widths[k - 1])
+        else:
+            pass_on(near_slot, 1)
+
+            @pl.when(pair + far < pairs)
+            def _():
+                state_copy(far_slot, near_slot, me + far_offset).start()
+
+    def begin_scan():
+        @pl.loop(0, half)
+        def _(h):
+            out_buf[0, h] = st_ref[other_half + h].astype(jnp.bfloat16)
+            dec_out[0, h] = dec_ref[other_half + h]
+
+        state_copy(0, 0, mate).start()
+        decay_copy(0, 0, mate).start()
+
+    def pair_stage():
+        state_copy(0, 0, mate).wait_recv()
+        decay_copy(0, 0, mate).wait_recv()
+
+        @pl.loop(0, half)
+        def _(h):
+            a, b = st_ref[mine + h], in_buf[0, h].astype(jnp.float32)
+            da, db = dec_ref[mine + h], dec_in[0, h]
+            low = core == 0
+            first, second = jnp.where(low, a, b), jnp.where(low, b, a)
+            d0, d1 = jnp.where(low, da, db), jnp.where(low, db, da)
+            lead[h] = first
+            dec_lead[h] = d0
+            t = d1[:1] * first + second
+            total[h] = t
+            dec_tot[h] = d0 * d1
+            out_buf[1, h] = t.astype(jnp.bfloat16)
+            dec_out[1, h] = d0 * d1
+
+        pass_to_all(1)
+
+    def double_stage(k):
+        @pl.when(pair >= widths[k - 1])
+        def _():
+            state_copy(k, k, mate).wait_recv()
+            decay_copy(k, k, mate).wait_recv()
+
+            @pl.loop(0, half)
+            def _(h):
+                d = dec_tot[h]
+                total[h] = total[h] + d[:1] * in_buf[k, h].astype(jnp.float32)
+                dec_tot[h] = d * dec_in[k, h]
+
+        @pl.loop(0, half)
+        def _(h):
+            out_buf[k + 1, h] = total[h].astype(jnp.bfloat16)
+            dec_out[k + 1, h] = dec_tot[h]
+
+        pass_to_all(k + 1)
+
+    def enter_stage():
+        @pl.loop(0, half)
+        def _(h):
+            total[h] = jnp.zeros(total.shape[1:], jnp.float32)
+
+        @pl.when(pair >= 1)
+        def _():
+            state_copy(near_slot, near_slot, mate).wait_recv()
+            decay_copy(near_slot, near_slot, mate).wait_recv()
+
+            @pl.loop(0, half)
+            def _(h):
+                total[h] = in_buf[near_slot, h].astype(jnp.float32)
+
+        @pl.when(pair >= far)
+        def _():
+            state_copy(far_slot, near_slot, mate).wait_recv()
+
+            @pl.loop(0, half)
+            def _(h):
+                total[h] = total[h] + dec_in[near_slot, h, :1] * in_buf[far_slot, h].astype(
+                    jnp.float32
+                )
+
+        @pl.loop(0, half)
+        def _(h):
+            enter = total[h]
+            second = dec_lead[h, :1] * enter + lead[h]
+            low = core == 0
+            in_ref[mine + h] = jnp.where(low, enter, second).astype(jnp.bfloat16)
+            out_buf[last_slot, h] = jnp.where(low, second, enter).astype(jnp.bfloat16)
+
+        state_copy(last_slot, last_slot, mate).start()
+
+    def finish_stage():
+        state_copy(last_slot, last_slot, mate).wait_recv()
+
+        @pl.loop(0, half)
+        def _(h):
+            in_ref[other_half + h] = in_buf[last_slot, h]
+
+    stages = [pair_stage]
+    stages += [functools.partial(double_stage, k) for k in range(1, near_slot)]
+    stages += [enter_stage, finish_stage]
+    all_steps = lines * groups
+
+    def finish_sends():
+        for k in (0, last_slot):
+            state_copy(k, k, mate).wait_send()
+        decay_copy(0, 0, mate).wait_send()
+        for k, distance in list(zip(range(1, near_slot), widths)) + [(near_slot, 1)]:
+
+            @pl.when(pair + distance < pairs)
+            def _():
+                state_copy(k, k, mate).wait_send()
+                decay_copy(k, k, mate).wait_send()
+
+        @pl.when(pair + far < pairs)
+        def _():
+            state_copy(far_slot, near_slot, mate).wait_send()
+
+    begin_scan()
 
     for g in range(groups):
         to_across(0, g, kv_ref.at[g]).start()
@@ -147,8 +293,7 @@
         pl.when(t < steps)(functools.partial(spread, t))
     relay(0)
 
-    @pl.loop(0, steps)
-    def _(s):
+    def step(s):
         pl.when((s + 2 < steps) & (s + 2 >= groups))(lambda: spread(s + 2))
         pl.when(s + 1 < steps)(lambda: relay(s + 1))
         age, g = s // groups, s % groups
@@ -157,6 +302,14 @@
         pl.when(age == 0)(lambda: work(0, g, True))
         pl.when(age > 0)(lambda: work(age, g, False))
 
+    @pl.loop(0, all_steps)
+    def _(s):
+        for k, stage in enumerate(stages):
+            pl.when(s == (k + 1) * all_steps // (len(stages) + 1))(stage)
+        pl.when(s < steps)(lambda: step(s))
+
+    finish_sends()
+
     @pl.loop(0, steps)
     def _(s):
         age, g = s // groups, s % groups
@@ -178,23 +331,43 @@
         ).astype(o_ref.dtype)
 
 
-def attend(kv, queries):
+def attend(kv, queries, local_state, block_decay):
     groups, rows, both = kv.shape
     lines = lax.axis_size("ctx") // ROW
     heads = queries.shape[1] // HEAD_WIDTH
+    pairs = lax.axis_size("ctx") // 2
+    widths = [1 << k for k in range(pairs.bit_length()) if 2 << k < pairs]
+    slots = len(widths) + 4
+    shape = (local_state.shape[0] // 2,) + local_state.shape[1:]
+    flat = (shape[0],) + block_decay.shape[1:]
+    slot_sems = pltpu.SemaphoreType.DMA((slots,))
     vmem = pl.BlockSpec(memory_space=pltpu.VMEM)
     sems = pltpu.SemaphoreType.DMA((lines, groups))
     return pl.pallas_call(
-        attend_kernel,
-        out_shape=jax.ShapeDtypeStruct(queries.shape, jnp.bfloat16),
-        in_specs=[vmem, vmem],
-        out_specs=vmem,
+        functools.partial(attend_kernel, widths),
+        out_shape=[
+            jax.ShapeDtypeStruct(queries.shape, jnp.bfloat16),
+            jax.ShapeDtypeStruct(local_state.shape, jnp.bfloat16),
+        ],
+        in_specs=[vmem] * 4,
+        out_specs=[vmem] * 2,
         scratch_shapes=[
             pltpu.VMEM((lines, groups, ROW * rows, both), jnp.bfloat16),
             pltpu.VMEM((heads, rows, HEAD_WIDTH), jnp.float32),
             pltpu.VMEM((heads, rows, 2 * HEAD_WIDTH), jnp.float32),
         ]
-        + [sems] * 8,
+        + [sems] * 8
+        + [
+            pltpu.VMEM((slots,) + shape, jnp.bfloat16),
+            pltpu.VMEM((slots,) + shape, jnp.bfloat16),
+            pltpu.VMEM((slots,) + flat, jnp.float32),
+            pltpu.VMEM((slots,) + flat, jnp.float32),
+            pltpu.VMEM(shape, jnp.float32),
+            pltpu.VMEM(shape, jnp.float32),
+            pltpu.VMEM(flat, jnp.float32),
+            pltpu.VMEM(flat, jnp.float32),
+        ]
+        + [slot_sems] * 4,
         compiler_params=pltpu.CompilerParams(
             vmem_limit_bytes=VMEM_LIMIT, collective_id=0, has_side_effects=True
         ),
@@ -204,7 +377,7 @@
             transcendentals=0,
         ),
         name="attend",
-    )(kv, queries)
+    )(kv, queries, local_state, block_decay)
 
 
 def pair_select(rows, first, second):
@@ -279,52 +452,6 @@
 def norm_kernel(count, g_ref, sq_ref, gain_ref, o_ref):
     scaling = lax.rsqrt(sq_ref[...] / count + 1e-05)
     o_ref[...] = (g_ref[...] * scaling * gain_ref[...].astype(jnp.float32)).astype(o_ref.dtype)
-
-
-def incoming_state(local_state, ends):
-    count = lax.axis_size("ctx")
-    position = lax.axis_index("ctx")
-    heads = local_state.shape[0]
-    half = heads // 2
-    core = position % 2
-    pair = position // 2
-    pairs = count // 2
-    all_ends = lax.all_gather(ends, "ctx")
-    low = core == 0
-    bf = jnp.bfloat16
-
-    sent = jnp.where(low, local_state[half:], local_state[:half]).astype(bf)
-    mine = jnp.where(low, local_state[:half], local_state[half:])
-    theirs = swapped(sent, "ctx").astype(jnp.float32)
-    ends_half = jnp.where(low, all_ends[:, :half], all_ends[:, half:])
-    pair_ends = ends_half.reshape(pairs, 2, half)
-    first = jnp.where(low, mine, theirs)
-    second = jnp.where(low, theirs, mine)
-    own = lax.dynamic_index_in_dim(pair_ends, pair, 0, keepdims=False)
-    pair_logs = pair_ends[:, 0] + pair_ends[:, 1]
-    index = jnp.arange(pairs)[:, None]
-
-    def window(last, width):
-        inside = (index > last - width) & (index <= last)
-        return jnp.exp(jnp.sum(jnp.where(inside, pair_logs, 0.0), axis=0))[:, None, None]
-
-    total = jnp.exp(own[1])[:, None, None] * first + second
-    width = 1
-    while 2 * width < pairs:
-        before = passed_along(total.astype(bf), "ctx", 2 * width).astype(jnp.float32)
-        total = total + window(pair, width) * before
-        width *= 2
-    packed = total.astype(bf)
-    near = passed_along(packed, "ctx", 2).astype(jnp.float32)
-    far = passed_along(packed, "ctx", 2 * (1 + width)).astype(jnp.float32)
-    enter = near + window(pair - 1, width) * far
-    enter_second = jnp.exp(own[0])[:, None, None] * enter + first
-    for_me = jnp.where(low, enter, enter_second).astype(bf)
-    for_them = jnp.where(low, enter_second, enter).astype(bf)
-    got = swapped(for_them, "ctx")
-    return jnp.where(
-        low, jnp.concatenate([for_me, got], axis=0), jnp.concatenate([got, for_me], axis=0)
-    )
 
 
 def local(
@@ -382,7 +509,10 @@
         name="local_state",
     )(ssm_input, b_matrix, columns(weight_end))
 
-    entering = incoming_state(local_state.reshape(heads, P_SIZE, N), ends)
+    block_decay = jnp.broadcast_to(jnp.exp(ends)[:, None, None], (heads, 8, N))
+    attention_out, entering = attend(
+        kv, queries, local_state.reshape(heads, P_SIZE, N), block_decay
+    )
 
     inner = pl.pallas_call(
         inner_kernel,
@@ -404,8 +534,6 @@
         by_group(step_size),
         jnp.repeat(skip_gain, P_SIZE)[None, :],
     )
-
-    attention_out = attend(kv, queries)
 
     gated, square = pl.pallas_call(
         gate_kernel,

time: 225 us -> 196 us (0.87)
  Pallas kernels: 126 us -> 164 us
  blocking collectives: 34.2 us -> 8.77 us
  waiting for transfers between devices: 22.4 us -> 0 us
  starting transfers between devices: 11.4 us -> 0 us
  other arithmetic: 9.77 us -> 2.6 us
    pallas_call x1, Pallas kernels: 105 us -> 143 us  [attend(): pl.pallas_call(functools.partial(attend_kernel, widths), out_shape=[jax.S...]
    unnamed x1 -> x0, blocking collectives: 24.4 us -> none
    ppermute x6 -> x0, waiting for transfers between devices: 22.4 us -> none  [the longest x4 22.4 us: passed_along(): return lax.ppermute(block, axis, route)]
    ppermute x6 -> x0, starting transfers between devices: 11.4 us -> none  [the longest x4 11.2 us: passed_along(): return lax.ppermute(block, axis, route)]
    convert_element_type x5 -> x0, other arithmetic: 6.48 us -> none  [the longest x1 2.81 us: incoming_state(): packed = total.astype(bf)]
    unnamed x42 -> x35, local copies, waits for them, and re-layouts: 10.5 us -> 11.7 us
  transfers between devices with their start and end apart: 6 -> 0, of which waited for: 2 -> 0; matrix products, arithmetic and copies ran while one was open for 5% -> 0% of each run, Pallas kernels for 50% -> 0%
where the time goes in v3:
time: 196 us; the launch traced here: 195 us
  Pallas kernels  164 us (84%)
  local copies, waits for them, and re-layouts  17.9 us (9%)
  blocking collectives  8.77 us (4%)
  other arithmetic  2.6 us (1%)
    pallas_call x1, Pallas kernels, attend(): pl.pallas_call(functools.partial(attend_kernel, widths), out_shape=[jax.S...  143 us
    unnamed x35, local copies, waits for them, and re-layouts  11.7 us
    psum x1, blocking collectives, local(): square = lax.psum(square, 'tp')  8.77 us
    pallas_call x1, Pallas kernels, local(): pl.pallas_call(inner_kernel, grid=(groups,), in_specs=[wide, narrow, narr...  6.77 us
    pallas_call x1, Pallas kernels, local(): pl.pallas_call(gate_kernel, grid=(groups,), in_specs=[wide, state, narrow...  6.43 us
    pallas_call x1, Pallas kernels, local(): pl.pallas_call(state_kernel, grid=(groups,), in_specs=[wide, narrow, colu...  5.52 us

profile of v3, /device:TPU:24, one launch (start us, length us, event | category | flops | bytes accessed | tf_op | source)
XLA Modules:
  0.0 195.0 jit_solution(11140628264966417906)
XLA Ops:
  0.6 0.0 copy-start
  0.6 1.0 stack.10
  1.7 0.4 copy.17
  2.1 0.0 copy-start.11
  2.1 1.0 stack.9
  3.2 0.0 copy-start.2
  3.2 0.0 copy-start.9
  3.2 0.4 copy.16
  3.6 1.9 maximum_bitcast_fusion
  5.5 1.4 reshape.36.kv_ref
  6.9 0.0 copy-done
  6.9 0.4 fusion
  7.3 0.2 slice_reduce_fusion
  7.4 0.0 copy-done.11
  7.5 0.7 bitcast_exponential_fusion
  8.2 1.0 copy.18
  9.2 0.0 copy-done.2
  9.2 0.0 copy-done.9
  9.2 0.0 copy-start.13
  9.2 5.5 %local_state.1 = f32[4096,128]{1,0:T(8,128)S(1)} custom-call(bf16[256,4096]{1,0:T(8,128)(2,1)S(1)} %copy-done.2, bf16[256,512]{1,0:T(8,128)(2,1)S(1)} %copy-done.9, f32[4,256,16]{2,1,0:T(8,128)S(1)} %bitcast.18), custom_call_target="tpu_custom_call" | custom-call | flops 1073741824 | bytes 4194304 | tf_op jit(solution)/shard_map/local_state/pallas_call | solution.py:499
  14.8 0.0 copy-start.5
  14.8 1.3 copy-done.5
  16.1 0.1 broadcast_in_dim.21.dec_ref
  16.2 0.0 copy-done.13
  16.2 0.0 copy-start.16
  16.3 143.4 %attend.1 = (bf16[256,4096]{1,0:T(8,128)(2,1)S(1)}, bf16[64,64,128]{2,1,0:T(8,128)(2,1)S(1)}) custom-call(bf16[4,256,256]{2,1,0:T(8,128)(2,1)S(1)} %reshape.36.kv_ref, bf16[256,4096]{1,0:T(8,128)(2,1)S(1)} %copy-done.13, f32[64,64,128]{2,1,0:T(8,128)} %bitcast.19, f32[64,8,128]{2,1,0:T(8,128)S(1)} %broadcast_in_dim.21.dec_ref), custom_call_target="tpu_custom_call" | custom-call | flops 42949672960 | bytes 8388608 | tf_op jit(solution)/shard_map/attend/pallas_call | solution.py:346
  159.7 0.0 copy-start.3
  159.7 1.3 copy-done.3
  161.0 1.0 copy-done.7
  162.0 0.2 copy.19.ccol_ref
  162.2 0.0 copy-done.16
  162.2 0.1 broadcast_in_dim.22
  162.3 0.1 broadcast_in_dim_reshape.3.skip_ref
  162.4 0.0 copy-start.10
  162.4 0.9 copy-done.10
  163.3 0.8 copy-done.12
  164.2 6.8 %inner.1.y_ref = f32[256,4096]{1,0:T(8,128)} custom-call(bf16[256,4096]{1,0:T(8,128)(2,1)S(1)} %copy-done.2, bf16[256,512]{1,0:T(8,128)(2,1)S(1)} %copy-done.9, bf16[256,512]{1,0:T(8,128)(2,1)S(1)} %copy-done.10, f32[4,256,16]{2,1,0:T(8,128)S(1)} %copy.19.ccol_ref, f32[4,16,256]{2,1,0:T(8,128)S(1)} %bitcast.23, f32[4,16,256]{2,1,0:T(8,128)S(1)} %bitcast.24, ...), custom_call_target="tpu_custom_call" | custom-call | flops 10737418240 | bytes 6291456 | tf_op jit(solution)/shard_map/inner/pallas_call | solution.py:517
  170.9 0.2 copy.20
  171.1 0.0 copy-start.6
  171.1 1.6 copy-done.6
  172.7 1.2 copy-done.8
  174.0 6.4 %gated.1 = (f32[256,4096]{1,0:T(8,128)}, f32[256,1]{1,0:T(8,128)S(1)}) custom-call(f32[256,4096]{1,0:T(8,128)} %inner.1.y_ref, bf16[4096,128]{1,0:T(8,128)(2,1)S(1)} %bitcast.20, bf16[256,512]{1,0:T(8,128)(2,1)S(1)} %copy-done.10, f32[4,256,16]{2,1,0:T(8,128)S(1)} %bitcast.17, bf16[256,4096]{1,0:T(8,128)(2,1)S(1)} %copy-done.6), custom_call_target="tpu_custom_call" | custom-call | flops 2147483648 | bytes 11534336 | tf_op jit(solution)/shard_map/gated/pallas_call | solution.py:538
  180.4 8.8 %psum.7.sq_ref = f32[256,1]{1,0:T(8,128)S(1)} all-reduce(f32[256,1]{1,0:T(8,128)S(1)} %get-tuple-element.9), channel_id=1, replica_groups=mesh['ctx'=16,'tp'=2] {'tp'}, use_global_device_ids=true, to_apply=%region_0.1 | all-reduce | flops 256 | bytes 2048 | tf_op jit(solution)/shard_map/psum | solution.py:553
  189.2 0.0 copy-start.1
  189.2 2.2 %copy-done.1 = f32[256,4096]{1,0:T(8,128)S(1)} copy-done((f32[256,4096]{1,0:T(8,128)S(1)}, f32[256,4096]{1,0:T(8,128)}, u32[]{:S(2)}) %copy-start.1) | copy-done | bytes 4194328
  191.4 2.3 %norm.1 = bf16[256,4096]{1,0:T(8,128)(2,1)} custom-call(f32[256,4096]{1,0:T(8,128)S(1)} %copy-done.1, f32[256,1]{1,0:T(8,128)S(1)} %psum.7.sq_ref, bf16[1,4096]{1,0:T(2,128)(2,1)S(1)} %broadcast_in_dim.23.gain_ref), custom_call_target="tpu_custom_call" | custom-call | tf_op jit(solution)/shard_map/norm/pallas_call | solution.py:554
  193.7 0.0 copy-done.4
  193.7 1.3 copy.22
  (11 shorter events, 0.0 us)
Async XLA Ops:
  0.6 6.3 %copy-start = (f32[64,256]{1,0:T(8,128)S(1)}, f32[64,256]{1,0:T(8,128)}, u32[]{:S(2)}) copy-start(f32[64,256]{1,0:T(8,128)} %param.19) | copy-start | bytes 196612
  2.1 5.3 %copy-start.11 = (f32[64,256]{1,0:T(8,128)S(1)}, f32[64,256]{1,0:T(8,128)}, u32[]{:S(2)}) copy-start(f32[64,256]{1,0:T(8,128)} %param.18) | copy-start | bytes 196612
  3.2 6.0 %copy-start.2 = (bf16[256,4096]{1,0:T(8,128)(2,1)S(1)}, bf16[256,4096]{1,0:T(8,128)(2,1)}, u32[]{:S(2)}) copy-start(bf16[256,4096]{1,0:T(8,128)(2,1)} %x_ref.3) | copy-start | bytes 6291460
  3.2 6.0 %copy-start.9 = (bf16[256,512]{1,0:T(8,128)(2,1)S(1)}, bf16[256,512]{1,0:T(8,128)(2,1)}, u32[]{:S(2)}) copy-start(bf16[256,512]{1,0:T(8,128)(2,1)} %b_ref.3) | copy-start | bytes 786436
  9.2 7.0 %copy-start.13 = (bf16[256,4096]{1,0:T(8,128)(2,1)S(1)}, bf16[256,4096]{1,0:T(8,128)(2,1)}, u32[]{:S(2)}) copy-start(bf16[256,4096]{1,0:T(8,128)(2,1)} %q_ref.1) | copy-start | bytes 6291460
  14.8 1.3 copy-start.5
  16.2 145.9 %copy-start.16 = (f32[64]{0:T(128)S(1)}, f32[64]{0:T(128)}, u32[]{:S(2)}) copy-start(f32[64]{0:T(128)} %param.20) | copy-start | bytes 772
  159.7 1.3 copy-start.3
  161.0 1.0 copy-start.7
  162.4 1.0 copy-start.10
  163.3 0.8 copy-start.12
  164.2 6.8 %copy-start.14 = (f32[64,256]{1,0:T(8,128)S(1)}, f32[64,256]{1,0:T(8,128)}, u32[]{:S(2)}) copy-start(f32[64,256]{1,0:T(8,128)} %get-tuple-element.10) | copy-start | bytes 196612
  171.1 1.6 copy-start.6
  172.7 1.2 copy-start.8
  174.0 15.2 %copy-start.15 = (bf16[4096]{0:T(1024)(128)(2,1)S(1)}, bf16[4096]{0:T(1024)(128)(2,1)}, u32[]{:S(2)}) copy-start(bf16[4096]{0:T(1024)(128)(2,1)} %param.21) | copy-start | bytes 24580
  189.2 2.2 %copy-start.1 = (f32[256,4096]{1,0:T(8,128)S(1)}, f32[256,4096]{1,0:T(8,128)}, u32[]{:S(2)}) copy-start(f32[256,4096]{1,0:T(8,128)} %get-tuple-element.8.g_ref) | copy-start | bytes 12582916
  191.4 2.3 %copy-start.4 = (bf16[256,4096]{1,0:T(8,128)(2,1)S(1)}, bf16[256,4096]{1,0:T(8,128)(2,1)}, u32[]{:S(2)}) copy-start(bf16[256,4096]{1,0:T(8,128)(2,1)} %copy-done.3) | copy-start | bytes 6291460
